TPU v7x, 32 devices: a whole 2x2x4 slice. The times are simulated.
32 devices in a mesh: src: 8 (over y, x, core), rcv: 4 (over z).
Axes of the slice: x: 2, y: 2, z: 4, core: 2. Of those that a mesh axis runs over, the one named last changes fastest.
Arguments:
- records: float32 [256, 20480], P(('rcv', 'src')), may hold values from -500 to 500
- starts: int32 [2], replicated, may hold values from 0 to 10180, as said below
- block_mask: int32 [4, 4, 8], P('rcv', None, 'src'), may hold values from 0 to 1, as said below
Outputs:
- stacked: bfloat16 [256, 4, 8, 8, 128], P('rcv', None, 'src')
Inputs may be any that keep to these rules, and one draw needn't show every extreme that they name: Some window starts at 10180. block_mask[a, b, c] is 0 wherever b < a.
All inputs are finite; a program needn't handle non-finite values.
Results may differ from a plain program's by a relative error of at most 0.0065.
Values may be sent and summed in bfloat16 or wider, within the bound.
A program may use at most 192 MiB of HBM per device.

v0:
```python
import math

import jax
import jax.numpy as jnp
from jax import lax
from jax.sharding import PartitionSpec as P

DEC = 5
KSEG = 13
NT = 2048
FB = 512
HALF = 64
LAGS = 128
TAPS = 65
F = 1024
RAW = 10300


eps_power = 1e-06


def from_behind(block, axis, distance):
    devices = range(lax.axis_size(axis))
    route = [((i - distance) % len(devices), i) for i in devices]
    return lax.ppermute(block, axis, route)


def lowpass():
    tap_index = jnp.arange(TAPS, dtype=jnp.float32)
    centre = (TAPS - 1) / 2.0
    taper = 0.5 - 0.5 * jnp.cos(2.0 * math.pi * (tap_index + 1.0) / (TAPS + 1.0))
    return jnp.sinc((tap_index - centre) / DEC) * taper / DEC


def decimate(windows):
    taps_kernel = lowpass()
    frames = windows.reshape(windows.shape[0], windows.shape[1], NT + KSEG - 1, DEC)
    traces = jnp.zeros((windows.shape[0], windows.shape[1], NT), jnp.float32)
    for segment in range(KSEG):
        weights = taps_kernel[segment * DEC : (segment + 1) * DEC]
        traces = traces + jnp.sum(frames[:, :, segment : segment + NT, :] * weights, axis=3)
    return traces


def smoother(bins, band, reach):
    source_bins = jnp.arange(bins, dtype=jnp.int32)[:, None]
    target_bins = jnp.arange(band, dtype=jnp.int32)[None, :]
    inside = jnp.abs(source_bins - target_bins) <= reach
    lowest = jnp.maximum(target_bins - reach, 0)
    highest = jnp.minimum(target_bins + reach, bins - 1)
    counted = (highest - lowest + 1).astype(jnp.float32)
    return jnp.where(inside, 1.0, 0.0).astype(jnp.float32) / counted


def fourier_table(samples, bins):
    sample_ids = jnp.arange(samples, dtype=jnp.int32)[:, None]
    bin_ids = jnp.arange(bins, dtype=jnp.int32)[None, :]
    phase_index = sample_ids * bin_ids % samples
    radians = 2.0 * math.pi / samples * phase_index.astype(jnp.float32)
    return jnp.concatenate([jnp.cos(radians), -jnp.sin(radians)], axis=1)


def whiten(records, starts):
    windows = jax.vmap(
        lambda window_start: lax.dynamic_slice_in_dim(records, window_start, RAW, 1)
    )(starts)
    traces = decimate(windows)
    used_bins = FB + HALF
    spectrum = jnp.dot(
        traces.reshape(-1, NT), fourier_table(NT, used_bins), precision=lax.Precision.HIGHEST
    )
    real_part = spectrum[:, :used_bins]
    imag_part = spectrum[:, used_bins:]
    power = real_part * real_part + imag_part * imag_part
    weights = smoother(F, FB, HALF)[:used_bins]
    smoothed = jnp.dot(power, weights, precision=lax.Precision.HIGHEST)
    divisor = jnp.sqrt(smoothed + eps_power)
    whitened = jnp.stack([real_part[:, :FB] / divisor, imag_part[:, :FB] / divisor], axis=1)
    whitened = whitened.reshape(traces.shape[0], traces.shape[1], 2, FB)
    return jnp.transpose(whitened, (1, 0, 2, 3)).astype(jnp.bfloat16)


def lag_table(band, lag_count, samples):
    bin_ids = jnp.arange(band, dtype=jnp.int32)[:, None]
    lag_ids = jnp.arange(lag_count, dtype=jnp.int32)[None, :] - lag_count // 2 + samples
    phase_index = bin_ids * lag_ids % samples
    radians = 2.0 * math.pi / samples * phase_index.astype(jnp.float32)
    return jnp.concatenate([jnp.cos(radians), -jnp.sin(radians)], axis=0).astype(jnp.bfloat16)


def correlate(sources, receivers, inverse):
    rotated = jnp.stack([-receivers[:, :, 1], receivers[:, :, 0]], axis=2)
    paired = jnp.stack([receivers, rotated], axis=1)
    cross = jnp.einsum("iwpf,jqwpf->ijqf", sources, paired, preferred_element_type=jnp.float32)
    cross = cross.astype(jnp.bfloat16)
    cross = cross.reshape(-1, 2 * cross.shape[3])
    return jnp.dot(cross, inverse, preferred_element_type=jnp.float32)


def on_device(records, starts, block_mask):
    own_spec = whiten(records, starts)
    piece_rows = own_spec.shape[0]
    sources = lax.all_gather(own_spec, "src", axis=0, tiled=True)
    block_rows = sources.shape[0]
    axis_count = lax.axis_size("rcv")
    inverse = lag_table(FB, LAGS, NT)
    normalizer = 1.0 / math.sqrt(own_spec.shape[1] * own_spec.shape[3])
    block_row = block_mask.reshape(-1)
    src_index = lax.axis_index("src")
    rcv_index = lax.axis_index("rcv")
    source_ids = rcv_index * block_rows + jnp.arange(block_rows, dtype=jnp.int32)
    pieces_all = jnp.arange(axis_count, dtype=jnp.int32)

    def evaluate(receivers, first_row):
        count_rows = receivers.shape[0]
        gathered = first_row + jnp.arange(count_rows, dtype=jnp.int32)
        position = gathered // piece_rows
        receiver_ids = position * block_rows + src_index * piece_rows + gathered % piece_rows
        allowed = jnp.sum(
            jnp.where(position[:, None] == pieces_all[None, :], block_row[None, :], 0), axis=1
        )
        lagged = (
            correlate(sources, receivers, inverse).reshape(block_rows, count_rows, LAGS)
            * normalizer
        )
        keep_pair = (source_ids[:, None] < receiver_ids[None, :]) & (allowed[None, :] > 0)
        return jnp.where(keep_pair[:, :, None], lagged, 0.0).astype(jnp.bfloat16)

    def place(result, receivers, position):
        wanted = jnp.sum(jnp.where(pieces_all == position, block_row, 0))

        def compute(held):
            return evaluate(held, position * piece_rows)

        def nothing(held):
            return jnp.zeros((block_rows, held.shape[0], LAGS), jnp.bfloat16)

        values = lax.cond(wanted > 0, compute, nothing, receivers)
        return lax.dynamic_update_slice(result, values[:, None], (0, position, 0, 0))

    result = jnp.zeros((block_rows, axis_count, piece_rows, LAGS), jnp.bfloat16)
    result = place(result, own_spec, rcv_index)

    def advance(turn_index, loop_state):
        holding, current = loop_state
        holding = from_behind(holding, "rcv", 1)
        return (holding, place(current, holding, (rcv_index - turn_index) % axis_count))

    _, result = lax.fori_loop(1, axis_count, advance, (own_spec, result))
    return result.reshape(block_rows, axis_count, 1, piece_rows, LAGS)


def solution(mesh):
    in_specs = (P(("rcv", "src"), None), P(), P("rcv", None, "src"))
    out_specs = P("rcv", None, "src", None, None)
    return jax.shard_map(
        on_device, mesh=mesh, in_specs=in_specs, out_specs=out_specs, check_vma=False
    )
```

profile of v0, /device:TPU:1, one launch (start us, length us, event | category | flops | bytes accessed | tf_op | source)
XLA Modules:
  0.0 216.0 jit_solution(2626099071612684994)
XLA Ops:
  1.0 5.0 %while.20 = (s32[]{:T(128)}, f32[8,20480]{1,0:T(8,128)}, s32[2,2]{1,0:T(2,128)S(1)}, f32[2,8,10300]{2,1,0:T(8,128)S(1)}, s32[]{:T(128)}) while((s32[]{:T(128)}, f32[8,20480]{1,0:T(8,128)}, s32[2,2]{1,0:T(2,128)S(1)}, f32[2,8,10300]{2,1,0:T(8,128)S(1)}, s32[]{:T(128)}) %tuple.122), condition=%wide.while_cond, body=%wide.while_body.sunk | while | flops 2 | bytes 661473 | solution.py:65
  6.0 15.9 %reshape.278 = f32[2,8,2060,5]{3,2,1,0:T(8,128)} reshape(f32[2,8,10300]{2,1,0:T(8,128)S(1)} %get-tuple-element.344) | data formatting | bytes 1318400 | tf_op jit(solution)/shard_map/reshape | solution.py:37
  21.9 56.5 %fusion.29 = (f32[2,8,2048]{2,1,0:T(8,128)S(1)}, f32[2,8,2048]{2,1,0:T(8,128)S(1)}, f32[2,8,2048]{2,1,0:T(8,128)S(1)}, f32[2,8,2048]{2,1,0:T(8,128)S(1)}, f32[2,...) fusion(f32[2,8,2060,5]{3,2,1,0:T(8,128)} %reshape.278, ...), kind=kLoop, calls=%fused_computation.74 | loop fusion | flops 2654208 | bytes 7078068 | tf_op jit(solution)/shard_map/reduce_sum | solution.py:41
  78.4 36.2 %fusion.30 = (f32[2,8,2048]{2,1,0:T(8,128)S(1)}, f32[2,8,2048]{2,1,0:T(8,128)S(1)}, f32[2,8,2048]{2,1,0:T(8,128)S(1)}, f32[2,8,2048]{2,1,0:T(8,128)S(1)}) fusion(f32[2,8,2060,5]{3,2,1,0:T(8,128)} %reshape.278, f32[5]{0:T(128)S(1)} %get-tuple-element.542, f32[5]{0:T(128)S(1)} %get-tuple-element.539, f32[5]{0:T(128)S(1)} %get-tuple-element.540, ...), kind=kLoop, calls=%fused_computation.76 | loop fusion | flops 1179648 | bytes 3145808 | tf_op jit(solution)/shard_map/reduce_sum | solution.py:41
  114.6 20.8 %sine_negate_fusion = (f32[2048,576]{1,0:T(8,128)S(1)}, f32[2048,576]{1,0:T(8,128)S(1)}) fusion(), kind=kLoop, calls=%fused_computation.87 | loop fusion | flops 17694720 | bytes 9437184 | tf_op jit(solution)/shard_map/neg | solution.py:60
  135.4 5.5 %fusion.31 = f32[16,1152]{1,0:T(8,128)S(1)} fusion(f32[2048,576]{1,0:T(8,128)S(1)} %get-tuple-element.543, f32[2048,576]{1,0:T(8,128)S(1)} %get-tuple-element.544, f32[2,8,2048]{2,1,0:T(8,128)S(1)} %get-tuple-element.476, f32[2,8,2048]{2,1,0:T(8,128)S(1)} %get-tuple-element.477, f32[2,8,2048]{2,1,0:T(8,128)S(1)} %get-tuple-element.478, ...), kind=kOutput, calls=%fused_computation.77 | convolution fusion | flops 455737344 | bytes 11214848 | tf_op jit(solution)/shard_map/dot_general | solution.py:69
  141.8 10.7 %all_gather.3 = bf16[64,2,2,512]{3,2,1,0:T(2,128)(2,1)S(1)} all-gather(bf16[8,2,2,512]{3,2,1,0:T(2,128)(2,1)S(1)} %maximum_bitcast_fusion.2), channel_id=1, replica_groups=mesh['src'=8,'rcv'=4] {'src'}, dimensions={0}, use_global_device_ids=true | all-gather | bytes 294912 | tf_op jit(solution)/shard_map/all_gather | solution.py:103
  155.6 10.7 %conditional.2 = (bf16[64,1,8,128]{3,2,0,1:T(8,128)(2,1)S(1)}) conditional(s32[]{:T(128)} %convert_element_type.62, () %tuple.43, (s32[]{:T(128)}, s32[]{:T(128)}, s32[]{:T(128)}, s32[4]{0:T(128)S(1)}, s32[1,4,1]{1,2,0:T(1,128)S(1)}, /*index=5*/bf16[8,2,2,512]{3,2,1,0:T(2,128)(2,1)S(1)}, bf16[64,2,2,512]{3,2,1,0:T(2,128)(2,1)S(1)}, ...), branch_computations={%region_14.15_spmd, %region_15.17_spmd} | conditional | flops 139191648 | bytes 7998492 | solution.py:138
  157.7 3.1 %fusion.4 = bf16[64,8,2,512]{0,1,2,3:T(8,128)(2,1)S(1)} fusion(bf16[8,2,2,2,512]{0,2,3,1,4:T(2,128)(2,1)S(1)} %copy.40, bf16[64,2,2,512,1]{0,1,2,4,3:T(2,128)(2,1)} %copy.53), kind=kOutput, calls=%fused_computation.3 | convolution fusion | flops 4718592 | bytes 1376256 | tf_op jit(solution)/shard_map/cond/branch_1_fun/iwpf,jqwpf->ijqf/dot_general | solution.py:94
  160.8 3.1 %copy.41 = bf16[64,8,2,512]{3,2,1,0:T(2,128)(2,1)S(1)} copy(bf16[64,8,2,512]{0,1,2,3:T(8,128)(2,1)S(1)} %fusion.4) | data formatting | bytes 2097152 | tf_op jit(solution)/shard_map/cond/branch_1_fun/convert_element_type | solution.py:95
  169.3 44.3 %while.21 = (s32[]{:T(128)}, bf16[8,2,2,512]{3,0,2,1:T(8,128)(2,1)S(1)}, bf16[64,4,8,128]{3,2,0,1:T(8,128)(2,1)}, s32[]{:T(128)}, s32[4]{0:T(128)S(1)}, /*index=...) while((s32[]{:T(128)}, ...), condition=%wide.region_22.23_spmd.clone.clone, body=%wide.region_17.22_spmd.clone.clone.sunk | while | flops 139191680 | bytes 7868134 | solution.py:149
  172.0 2.0 collective-permute-done
  174.0 9.5 %conditional.6 = (bf16[64,1,8,128]{3,2,0,1:T(8,128)(2,1)S(1)}) conditional(s32[]{:T(128)} %convert_element_type.94, () %tuple.120, (s32[]{:T(128)}, s32[]{:T(128)}, s32[]{:T(128)}, s32[4]{0:T(128)S(1)}, s32[1,4,1]{1,2,0:T(1,128)S(1)}, /*index=5*/bf16[8,2,2,512]{3,0,2,1:T(8,128)(2,1)S(1)}, bf16[64,2,2,512]{0,1,2,3:T(2,128)(2,1)}, ...), branch_computations={%region_19.19_spmd, %region_20.21_spmd} | conditional | flops 139191648 | bytes 7408668 | solution.py:138
  174.8 3.1 %fusion.10 = bf16[64,8,2,512]{0,1,2,3:T(8,128)(2,1)S(1)} fusion(bf16[8,2,2,2,512]{0,2,3,1,4:T(2,128)(2,1)S(1)} %copy.43, bf16[64,2,2,512]{0,1,2,3:T(2,128)(2,1)} %get-tuple-element.320), kind=kOutput, calls=%fused_computation.25 | convolution fusion | flops 4718592 | bytes 1376256 | tf_op jit(solution)/shard_map/while/body/eval_jaxpr/cond/branch_1_fun/iwpf,jqwpf->ijqf/dot_general | solution.py:94
  177.9 3.1 %copy.44 = bf16[64,8,2,512]{3,2,1,0:T(2,128)(2,1)S(1)} copy(bf16[64,8,2,512]{0,1,2,3:T(8,128)(2,1)S(1)} %fusion.10) | data formatting | bytes 2097152 | tf_op jit(solution)/shard_map/while/body/eval_jaxpr/cond/branch_1_fun/convert_element_type | solution.py:95
  185.5 3.2 %collective-permute-done = bf16[8,2,2,512]{3,0,2,1:T(8,128)(2,1)S(1)} collective-permute-done((bf16[8,2,2,512]{3,0,2,1:T(8,128)(2,1)S(1)}, bf16[8,2,2,512]{3,0,2,1:T(8,128)(2,1)S(1)}, u32[]{:S(2)}, u32[]{:S(2)}) %collective-permute-start) | collective-permute-done | bytes 32800 | tf_op jit(solution)/shard_map/while/body/eval_jaxpr/ppermute | solution.py:25
  188.7 9.5 %conditional.6 = (bf16[64,1,8,128]{3,2,0,1:T(8,128)(2,1)S(1)}) conditional(s32[]{:T(128)} %convert_element_type.94, () %tuple.120, (s32[]{:T(128)}, s32[]{:T(128)}, s32[]{:T(128)}, s32[4]{0:T(128)S(1)}, s32[1,4,1]{1,2,0:T(1,128)S(1)}, /*index=5*/bf16[8,2,2,512]{3,0,2,1:T(8,128)(2,1)S(1)}, bf16[64,2,2,512]{0,1,2,3:T(2,128)(2,1)}, ...), branch_computations={%region_19.19_spmd, %region_20.21_spmd} | conditional | flops 139191648 | bytes 7408668 | solution.py:138
  189.5 3.1 %fusion.10 = bf16[64,8,2,512]{0,1,2,3:T(8,128)(2,1)S(1)} fusion(bf16[8,2,2,2,512]{0,2,3,1,4:T(2,128)(2,1)S(1)} %copy.43, bf16[64,2,2,512]{0,1,2,3:T(2,128)(2,1)} %get-tuple-element.320), kind=kOutput, calls=%fused_computation.25 | convolution fusion | flops 4718592 | bytes 1376256 | tf_op jit(solution)/shard_map/while/body/eval_jaxpr/cond/branch_1_fun/iwpf,jqwpf->ijqf/dot_general | solution.py:94
  192.6 3.1 %copy.44 = bf16[64,8,2,512]{3,2,1,0:T(2,128)(2,1)S(1)} copy(bf16[64,8,2,512]{0,1,2,3:T(8,128)(2,1)S(1)} %fusion.10) | data formatting | bytes 2097152 | tf_op jit(solution)/shard_map/while/body/eval_jaxpr/cond/branch_1_fun/convert_element_type | solution.py:95
  200.2 3.2 %collective-permute-done = bf16[8,2,2,512]{3,0,2,1:T(8,128)(2,1)S(1)} collective-permute-done((bf16[8,2,2,512]{3,0,2,1:T(8,128)(2,1)S(1)}, bf16[8,2,2,512]{3,0,2,1:T(8,128)(2,1)S(1)}, u32[]{:S(2)}, u32[]{:S(2)}) %collective-permute-start) | collective-permute-done | bytes 32800 | tf_op jit(solution)/shard_map/while/body/eval_jaxpr/ppermute | solution.py:25
  203.5 9.5 %conditional.6 = (bf16[64,1,8,128]{3,2,0,1:T(8,128)(2,1)S(1)}) conditional(s32[]{:T(128)} %convert_element_type.94, () %tuple.120, (s32[]{:T(128)}, s32[]{:T(128)}, s32[]{:T(128)}, s32[4]{0:T(128)S(1)}, s32[1,4,1]{1,2,0:T(1,128)S(1)}, /*index=5*/bf16[8,2,2,512]{3,0,2,1:T(8,128)(2,1)S(1)}, bf16[64,2,2,512]{0,1,2,3:T(2,128)(2,1)}, ...), branch_computations={%region_19.19_spmd, %region_20.21_spmd} | conditional | flops 139191648 | bytes 7408668 | solution.py:138
  204.3 3.1 %fusion.10 = bf16[64,8,2,512]{0,1,2,3:T(8,128)(2,1)S(1)} fusion(bf16[8,2,2,2,512]{0,2,3,1,4:T(2,128)(2,1)S(1)} %copy.43, bf16[64,2,2,512]{0,1,2,3:T(2,128)(2,1)} %get-tuple-element.320), kind=kOutput, calls=%fused_computation.25 | convolution fusion | flops 4718592 | bytes 1376256 | tf_op jit(solution)/shard_map/while/body/eval_jaxpr/cond/branch_1_fun/iwpf,jqwpf->ijqf/dot_general | solution.py:94
  207.4 3.1 %copy.44 = bf16[64,8,2,512]{3,2,1,0:T(2,128)(2,1)S(1)} copy(bf16[64,8,2,512]{0,1,2,3:T(8,128)(2,1)S(1)} %fusion.10) | data formatting | bytes 2097152 | tf_op jit(solution)/shard_map/while/body/eval_jaxpr/cond/branch_1_fun/convert_element_type | solution.py:95
  213.6 1.9 copy.64
  (97 shorter events, 31.8 us)
Async XLA Ops:
  140.9 13.4 %copy-start = (s32[1,4,1]{1,2,0:T(1,128)S(1)}, s32[1,4,1]{1,2,0:T(1,128)}, u32[]{:S(2)}) copy-start(s32[1,4,1]{1,2,0:T(1,128)} %param.11) | copy-start | bytes 52
  169.3 4.7 %collective-permute-start = (bf16[8,2,2,512]{3,0,2,1:T(8,128)(2,1)S(1)}, bf16[8,2,2,512]{3,0,2,1:T(8,128)(2,1)S(1)}, u32[]{:S(2)}, u32[]{:S(2)}) collective-permute-start(bf16[8,2,2,512]{3,0,2,1:T(8,128)(2,1)S(1)} %get-tuple-element.661), channel_id=1, source_target_pairs={{3,0},{0,1},{1,2},{2,3},{7,4},{4,5},{5,6},{6,7},{11,8},{8,9},{9,10... | collective-permute-start | bytes 98312 | tf_op jit(solution)/shard_map/while/body/eval_jaxpr/ppermute | solution.py:25
  184.2 4.6 %collective-permute-start = (bf16[8,2,2,512]{3,0,2,1:T(8,128)(2,1)S(1)}, bf16[8,2,2,512]{3,0,2,1:T(8,128)(2,1)S(1)}, u32[]{:S(2)}, u32[]{:S(2)}) collective-permute-start(bf16[8,2,2,512]{3,0,2,1:T(8,128)(2,1)S(1)} %get-tuple-element.661), channel_id=1, source_target_pairs={{3,0},{0,1},{1,2},{2,3},{7,4},{4,5},{5,6},{6,7},{11,8},{8,9},{9,10... | collective-permute-start | bytes 98312 | tf_op jit(solution)/shard_map/while/body/eval_jaxpr/ppermute | solution.py:25
  198.9 4.6 %collective-permute-start = (bf16[8,2,2,512]{3,0,2,1:T(8,128)(2,1)S(1)}, bf16[8,2,2,512]{3,0,2,1:T(8,128)(2,1)S(1)}, u32[]{:S(2)}, u32[]{:S(2)}) collective-permute-start(bf16[8,2,2,512]{3,0,2,1:T(8,128)(2,1)S(1)} %get-tuple-element.661), channel_id=1, source_target_pairs={{3,0},{0,1},{1,2},{2,3},{7,4},{4,5},{5,6},{6,7},{11,8},{8,9},{9,10... | collective-permute-start | bytes 98312 | tf_op jit(solution)/shard_map/while/body/eval_jaxpr/ppermute | solution.py:25
where the time goes:
time: 218 us; the launch traced here: 216 us
  other arithmetic  120 us (55%)
  local copies, waits for them, and re-layouts  48.2 us (22%)
  matrix products  24.1 us (11%)
  blocking collectives  10.7 us (5%)
  waiting for transfers between devices  8.5 us (4%)
  loops' own time  2.27 us (1%)
    reduce_sum x2, other arithmetic, decimate(): jnp.sum(frames[:, :, segment:segment + NT, :] * weights, axis=3)  92.7 us
    neg x1, other arithmetic, fourier_table(): return jnp.concatenate([jnp.cos(radians), -jnp.sin(radians)], axis=1)  20.8 us
    reshape x1, local copies, waits for them, and re-layouts, decimate(): windows.reshape(windows.shape[0], windows.shape[1], NT + KSEG - 1, DEC)  15.9 us
    convert_element_type x4, local copies, waits for them, and re-layouts, correlate(): cross = cross.astype(jnp.bfloat16)  12.4 us
    dot_general x4, matrix products, correlate(): jnp.einsum('iwpf,jqwpf->ijqf', sources, paired, preferred_element_type=jn...  12.3 us
    all_gather x1, blocking collectives, on_device(): sources = lax.all_gather(own_spec, 'src', axis=0, tiled=True)  10.7 us
    ppermute x3, waiting for transfers between devices, from_behind(): return lax.ppermute(block, axis, route)  8.5 us
    dot_general x4, matrix products, correlate(): return jnp.dot(cross, inverse, preferred_element_type=jnp.float32)  5.57 us
  transfers between devices with their start and end apart: 3, of which 3 were waited for; matrix products, arithmetic and copies ran while one was open for 1% of the time, Pallas kernels for 0%

commit v1 on v0

v1 whole, which is shorter than its diff:
```python
import functools
import math

import jax
import jax.numpy as jnp
import ml_dtypes
import numpy as np
from jax import lax
from jax.experimental import pallas as pl
from jax.experimental.pallas import tpu as pltpu
from jax.sharding import PartitionSpec as P

DEC = 5
NT = 2048
FB = 512
HALF = 64
LAGS = 128
TAPS = 65
F = 1024
LANES = 128
WINDOWS = 2
CH = 8

CHUNKS = NT // LANES
STRIDE = DEC * LANES
SPAN = 7 * LANES
RESID = 200
SUB_BINS = FB // CHUNKS
MORE_BINS = HALF // CHUNKS
GROUPS = CHUNKS // 2

eps_power = 1e-06
MESH = pl.DeviceIdType.MESH


def residues(group):
    return (0, CHUNKS // 2) if group == 0 else (group, CHUNKS - group)


def halves(table):
    high = table.astype(ml_dtypes.bfloat16)
    low = (table - high.astype(np.float64)).astype(ml_dtypes.bfloat16)
    return np.stack([high, low])


def band_matrix():
    tap = np.arange(TAPS, dtype=np.float64)
    taper = 0.5 - 0.5 * np.cos(2.0 * math.pi * (tap + 1.0) / (TAPS + 1.0))
    taps = np.sinc((tap - (TAPS - 1) / 2.0) / DEC) * taper / DEC
    k = np.arange(SPAN + RESID)[:, None] - RESID - DEC * np.arange(LANES)[None, :]
    return np.where((k >= 0) & (k < TAPS), taps[np.clip(k, 0, TAPS - 1)], 0.0).astype(np.float32)


def transform_tables():
    n0 = np.arange(LANES)[:, None]
    tables = np.zeros((GROUPS, 2 * LANES, 2 * LANES))
    band = np.zeros(FB, np.int64)
    beyond = np.zeros(LANES, np.int64)
    for g in range(GROUPS):
        re_at, im_at = (0, LANES // 2) if g % 2 == 0 else (LANES // 2, 0)
        for which, f0 in enumerate(residues(g)):
            for f1 in range(SUB_BINS + MORE_BINS):
                f = CHUNKS * f1 + f0
                if f1 < SUB_BINS:
                    col_re = re_at + which * SUB_BINS + f1
                    col_im = im_at + which * SUB_BINS + f1
                    band[g * 2 * SUB_BINS + which * SUB_BINS + f1] = f
                else:
                    lane = g * 2 * MORE_BINS + which * MORE_BINS + f1 - SUB_BINS
                    col_re = LANES + lane
                    col_im = LANES + LANES // 2 + lane
                    beyond[lane] = beyond[LANES // 2 + lane] = f
                phase = 2.0 * math.pi / NT * (n0[:, 0] * f % NT)
                cos, sin = np.cos(phase), np.sin(phase)
                if g == 0:
                    rows = slice(which * LANES, (which + 1) * LANES)
                    tables[g, rows, col_re] = cos
                    tables[g, rows, col_im] = -sin
                else:
                    sign = 1.0 if which == 0 else -1.0
                    tables[g, :LANES, col_re] = cos
                    tables[g, LANES:, col_re] = sign * sin
                    tables[g, :LANES, col_im] = -sin
                    tables[g, LANES:, col_im] = sign * cos
    return tables, band, beyond


def constants():
    tables, band, beyond = transform_tables()
    source = np.concatenate([band, beyond])[:, None]
    inside = (np.abs(source - band[None, :]) <= HALF).astype(ml_dtypes.bfloat16)
    count = np.minimum(band + HALF, F - 1) - np.maximum(band - HALF, 0) + 1
    per_bin = (1.0 / count).astype(np.float32)[None, :]
    phase = 2.0 * math.pi / NT * (band[:, None] * (np.arange(LAGS)[None, :] - LAGS // 2 + NT) % NT)
    lags = np.concatenate([np.cos(phase), -np.sin(phase)]).astype(np.float32)
    lags = lags.astype(ml_dtypes.bfloat16).astype(np.float32) / math.sqrt(WINDOWS * FB)
    return band_matrix(), halves(tables), inside, per_bin, lags.astype(ml_dtypes.bfloat16)


def real_dft(x):
    n = len(x)
    if n == 2:
        return [(x[0] + x[1], None), (x[0] - x[1], None)]
    half = n // 2
    even = real_dft([x[b] + x[b + half] for b in range(half)])
    odd = [x[b] - x[b + half] for b in range(half)]
    out = [None] * (half + 1)
    out[::2] = even
    for f in range(1, half, 2):
        re = odd[0]
        im = odd[half // 2] * -math.sin(math.pi * f / 2)
        for b in range(1, half // 2):
            re = re + (odd[b] - odd[half - b]) * math.cos(2 * math.pi * f * b / n)
            im = im - (odd[b] + odd[half - b]) * math.sin(2 * math.pi * f * b / n)
        out[f] = (re, im)
    return out


def split(x):
    high = x.astype(jnp.bfloat16)
    return high, (x - high.astype(jnp.float32)).astype(jnp.bfloat16)


def dot(a, b):
    return jnp.dot(a, b, preferred_element_type=jnp.float32)


def both_halves(x, table_high, table_low):
    rows = x.shape[0]
    high, low = split(x)
    top = dot(jnp.concatenate([high, low], axis=0), table_high)
    return top[:rows] + top[rows:] + dot(high, table_low)


def flip(index, mask, bits):
    for b in range(bits):
        bit = 1 << b
        index = index + (mask // bit % 2) * bit * (1 - 2 * (index // bit % 2))
    return index


def whiten(starts, records, band, tables, inside, per_bin, waits):
    traces = []
    for w in range(WINDOWS):
        start = starts[w]
        last = records.shape[1] - STRIDE * (CHUNKS - 1) - SPAN
        base = jnp.minimum(start // LANES * LANES, last)
        if w == 0:
            waits[0]()
        raw = jnp.concatenate(
            [
                records[:, pl.ds(pl.multiple_of(base + STRIDE * b, LANES), SPAN)]
                for b in range(CHUNKS)
            ],
            axis=0,
        )
        taps_high, taps_low = split(band[pl.ds(RESID - (start - base), SPAN), :])
        traces.append(both_halves(raw, taps_high, taps_low))
    pieces = [
        jnp.concatenate([t[CH * b : CH * (b + 1)] for t in traces], axis=0) for b in range(CHUNKS)
    ]
    bins = real_dft(pieces)
    waits[1]()
    outs = []
    for g in range(GROUPS):
        if g == 0:
            x = jnp.concatenate([bins[0][0], bins[CHUNKS // 2][0]], axis=1)
        else:
            x = jnp.concatenate(bins[g], axis=1)
        outs.append(both_halves(x, tables[0, g], tables[1, g]))
    beyond = functools.reduce(lambda a, b: a + b, [o[:, LANES:] for o in outs])
    first = lax.broadcasted_iota(jnp.int32, (WINDOWS * CH, LANES), 1) < LANES // 2
    re, im = [], []
    for q in range(GROUPS // 2):
        a, b = outs[2 * q][:, :LANES], outs[2 * q + 1][:, :LANES]
        re.append(jnp.where(first, a, b))
        im.append(pltpu.roll(jnp.where(first, b, a), LANES // 2, 1))
    re, im = jnp.concatenate(re, axis=1), jnp.concatenate(im, axis=1)
    power = jnp.concatenate([re * re + im * im, beyond * beyond], axis=1)
    waits[2]()
    both = dot(jnp.concatenate(split(power), axis=0), inside[...])
    smoothed = (both[: WINDOWS * CH] + both[WINDOWS * CH :]) * per_bin[...]
    scale = lax.rsqrt(smoothed + eps_power)
    return jnp.concatenate([re * scale, im * scale], axis=1).astype(jnp.bfloat16)


def spectra_kernel(
    starts, per_bin, records_hbm, band_hbm, tables_hbm, inside_hbm, out,
    records, band, tables, inside, load_sem,
):
    loads = [
        pltpu.make_async_copy(a, b, load_sem.at[i])
        for i, (a, b) in enumerate(
            [(records_hbm, records), (band_hbm, band), (tables_hbm, tables), (inside_hbm, inside)]
        )
    ]
    for load in loads:
        load.start()

    def first_wait():
        loads[0].wait()
        loads[1].wait()

    out[...] = whiten(
        starts, records, band, tables, inside, per_bin, [first_wait, loads[2].wait, loads[3].wait]
    )


def pair_kernel(
    n_src, n_rcv, mask, own, lags_hbm, out,
    lags, src_buf, rcv_buf, src_f32, rcv_f32, cross, threshold,
    load_sem, src_send, src_recv, rcv_send, rcv_recv,
):
    me_s, me_r = lax.axis_index("src"), lax.axis_index("rcv")
    src_bits, rcv_bits = n_src.bit_length() - 1, n_rcv.bit_length() - 1
    load = pltpu.make_async_copy(lags_hbm, lags, load_sem)
    load.start()

    barrier = pltpu.get_barrier_semaphore()

    def greet_src(k, _):
        peer = flip(me_s, k, src_bits)
        pl.semaphore_signal(barrier, inc=1, device_id={"src": peer}, device_id_type=MESH)
        return 0

    def greet_rcv(k, _):
        peer = flip(me_r, k, rcv_bits)
        pl.semaphore_signal(barrier, inc=1, device_id={"rcv": peer}, device_id_type=MESH)
        return 0

    lax.fori_loop(1, n_src, greet_src, 0)
    lax.fori_loop(1, n_rcv, greet_rcv, 0)

    src_buf[me_s] = own[...]
    rcv_buf[me_r] = own[...]
    pl.semaphore_wait(barrier, n_src + n_rcv - 2)

    def src_copy(slot, peer):
        return pltpu.make_async_remote_copy(
            src_ref=src_buf.at[slot], dst_ref=src_buf.at[slot], send_sem=src_send.at[peer],
            recv_sem=src_recv.at[slot], device_id={"src": peer}, device_id_type=MESH,
        )

    def rcv_copy(slot, peer):
        return pltpu.make_async_remote_copy(
            src_ref=rcv_buf.at[slot], dst_ref=rcv_buf.at[slot], send_sem=rcv_send.at[peer],
            recv_sem=rcv_recv.at[slot], device_id={"rcv": peer}, device_id_type=MESH,
        )

    def send_rcv(k, _):
        rcv_copy(me_r, flip(me_r, k, rcv_bits)).start()
        return 0

    def send_src(k, _):
        src_copy(me_s, flip(me_s, k, src_bits)).start()
        return 0

    lax.fori_loop(1, n_rcv, send_rcv, 0)
    lax.fori_loop(1, n_src, send_src, 0)

    block_rows = n_src * CH
    for b in range(n_rcv):
        ids = lax.broadcasted_iota(jnp.int32, (CH, LAGS), 0) + b * block_rows + me_s * CH
        threshold[CH * b : CH * (b + 1), :] = jnp.where(mask[0, b, 0] > 0, ids, -1)

    def land_rcv(k, _):
        peer = flip(me_r, k, rcv_bits)

        @pl.when(k > 0)
        def _():
            rcv_copy(peer, peer).wait_recv()

        held = rcv_buf[peer].astype(jnp.float32)
        for w in range(WINDOWS):
            rcv_f32[w, pl.ds(pl.multiple_of(peer * CH, CH), CH), :] = held[w * CH : (w + 1) * CH]
        return 0

    lax.fori_loop(0, n_rcv, land_rcv, 0)
    load.wait()

    rows = n_rcv * CH
    part = min(rows, 32)

    def per_source(k, _):
        peer = flip(me_s, k, src_bits)

        @pl.when(k > 0)
        def _():
            src_copy(peer, peer).wait_recv()

        src_f32[...] = src_buf[peer].astype(jnp.float32)
        for at in range(0, rows, part):
            for q in range(FB // LANES):
                lo, hi = q * LANES, FB + q * LANES
                held = [
                    (rcv_f32[w, at : at + part, lo : lo + LANES], rcv_f32[w, at : at + part, hi : hi + LANES])
                    for w in range(WINDOWS)
                ]
                for c in range(CH):
                    re = im = None
                    for w in range(WINDOWS):
                        row = w * CH + c
                        s_re = src_f32[row : row + 1, lo : lo + LANES]
                        s_im = src_f32[row : row + 1, hi : hi + LANES]
                        r_re, r_im = held[w]
                        one = s_re * r_re + s_im * r_im
                        two = s_im * r_re - s_re * r_im
                        re = one if re is None else re + one
                        im = two if im is None else im + two
                    to = c * rows + at
                    cross[to : to + part, lo : lo + LANES] = re.astype(jnp.bfloat16)
                    cross[to : to + part, hi : hi + LANES] = im.astype(jnp.bfloat16)
        lagged = dot(cross[...], lags[...])
        first_id = me_r * block_rows + peer * CH
        for c in range(CH):
            keep = threshold[...] > first_id + c
            value = jnp.where(keep, lagged[c * rows : (c + 1) * rows], 0.0)
            out[peer * CH + c] = value.astype(jnp.bfloat16)
        return 0

    lax.fori_loop(0, n_src, per_source, 0)

    def sent_src(k, _):
        src_copy(me_s, flip(me_s, k, src_bits)).wait_send()
        return 0

    def sent_rcv(k, _):
        rcv_copy(me_r, flip(me_r, k, rcv_bits)).wait_send()
        return 0

    lax.fori_loop(1, n_src, sent_src, 0)
    lax.fori_loop(1, n_rcv, sent_rcv, 0)


def on_device(n_src, n_rcv, records, starts, block_mask):
    band, tables, inside, per_bin, lags = constants()
    rows = n_rcv * CH
    held = (WINDOWS * CH, 2 * FB)
    smem = pl.BlockSpec(memory_space=pltpu.SMEM)
    vmem = pl.BlockSpec(memory_space=pltpu.VMEM)
    anywhere = pl.BlockSpec(memory_space=pl.ANY)
    own = pl.pallas_call(
        spectra_kernel,
        out_shape=jax.ShapeDtypeStruct(held, jnp.bfloat16),
        in_specs=[smem, vmem] + [anywhere] * 4,
        out_specs=vmem,
        scratch_shapes=[
            pltpu.VMEM(records.shape, jnp.float32),
            pltpu.VMEM(band.shape, jnp.float32),
            pltpu.VMEM(tables.shape, jnp.bfloat16),
            pltpu.VMEM(inside.shape, jnp.bfloat16),
            pltpu.SemaphoreType.DMA((4,)),
        ],
        compiler_params=pltpu.CompilerParams(vmem_limit_bytes=32 * 1024 * 1024),
    )(starts, per_bin, records, band, tables, inside)
    result = pl.pallas_call(
        functools.partial(pair_kernel, n_src, n_rcv),
        out_shape=jax.ShapeDtypeStruct((n_src * CH, rows, LAGS), jnp.bfloat16),
        in_specs=[smem, vmem, anywhere],
        out_specs=vmem,
        scratch_shapes=[
            pltpu.VMEM(lags.shape, jnp.bfloat16),
            pltpu.VMEM((n_src,) + held, jnp.bfloat16),
            pltpu.VMEM((n_rcv,) + held, jnp.bfloat16),
            pltpu.VMEM(held, jnp.float32),
            pltpu.VMEM((WINDOWS, rows, 2 * FB), jnp.float32),
            pltpu.VMEM((CH * rows, 2 * FB), jnp.bfloat16),
            pltpu.VMEM((rows, LAGS), jnp.int32),
            pltpu.SemaphoreType.DMA,
            pltpu.SemaphoreType.DMA((n_src,)),
            pltpu.SemaphoreType.DMA((n_src,)),
            pltpu.SemaphoreType.DMA((n_rcv,)),
            pltpu.SemaphoreType.DMA((n_rcv,)),
        ],
        compiler_params=pltpu.CompilerParams(
            collective_id=0, has_side_effects=True, vmem_limit_bytes=32 * 1024 * 1024
        ),
    )(block_mask, own, lags)
    return result.reshape(n_src * CH, n_rcv, 1, CH, LAGS)


def solution(mesh):
    in_specs = (P(("rcv", "src"), None), P(), P("rcv", None, "src"))
    out_specs = P("rcv", None, "src", None, None)
    return jax.shard_map(
        functools.partial(on_device, mesh.shape["src"], mesh.shape["rcv"]),
        mesh=mesh, in_specs=in_specs, out_specs=out_specs, check_vma=False,
    )
```

time: 218 us -> 27.5 us (0.13)
  the two profiles are of different devices: /device:TPU:1 before, /device:TPU:0 now
where the time goes in v1:
time: 27.5 us; the launch traced here: 27.2 us
  Pallas kernels  19.5 us (71%)
  local copies, waits for them, and re-layouts  7.69 us (28%)
    pallas_call x1, Pallas kernels, on_device(): pl.pallas_call(functools.partial(pair_kernel, n_src, n_rcv), out_shape=ja...  17 us
    unnamed x16, local copies, waits for them, and re-layouts  7.69 us
    pallas_call x1, Pallas kernels, on_device(): pl.pallas_call(spectra_kernel, out_shape=jax.ShapeDtypeStruct(held, jnp.b...  2.54 us

profile of v1, /device:TPU:0, one launch (start us, length us, event | category | flops | bytes accessed | tf_op | source)
XLA Modules:
  0.0 27.2 jit_solution(8943476118447613621)
XLA Ops:
  0.0 0.7 %copy.9.mask = s32[1,4,1]{2,1,0:T(4,128)S(1)} copy(s32[1,4,1]{1,2,0:T(1,128)} %param.10) | data formatting | bytes 32 | tf_op args[2]
  0.7 0.0 copy-start
  0.7 1.6 %copy-done = bf16[2,8,256,256]{3,2,1,0:T(8,128)(2,1)S(1)} copy-done((bf16[2,8,256,256]{3,2,1,0:T(8,128)(2,1)S(1)}, bf16[2,8,256,256]{3,2,1,0:T(8,128)(2,1)}, u32[]{:S(2)}) %copy-start) | copy-done | bytes 2097176
  2.3 0.0 copy-start.1
  2.3 1.1 %copy-done.1 = f32[8,20480]{1,0:T(8,128)S(1)} copy-done((f32[8,20480]{1,0:T(8,128)S(1)}, f32[8,20480]{1,0:T(8,128)}, u32[]{:S(2)}) %copy-start.1) | copy-done | bytes 655384
  3.4 0.0 copy-start.2
  3.4 1.1 %copy-done.2 = bf16[640,512]{1,0:T(8,128)(2,1)S(1)} copy-done((bf16[640,512]{1,0:T(8,128)(2,1)S(1)}, bf16[640,512]{1,0:T(8,128)(2,1)}, u32[]{:S(2)}) %copy-start.2) | copy-done | bytes 655384
  4.5 0.0 copy-start.3
  4.5 1.1 %copy-done.3 = f32[1096,128]{1,0:T(8,128)S(1)} copy-done((f32[1096,128]{1,0:T(8,128)S(1)}, f32[1096,128]{1,0:T(8,128)}, u32[]{:S(2)}) %copy-start.3) | copy-done | bytes 561176
  5.6 0.0 copy-start.5
  5.6 0.7 %copy-done.5 = f32[1,512]{1,0:T(1,128)S(1)} copy-done((f32[1,512]{1,0:T(1,128)S(1)}, f32[1,512]{1,0:T(1,128)}, u32[]{:S(2)}) %copy-start.5) | copy-done | bytes 2072
  6.2 0.0 copy-start.6
  6.2 0.7 %copy-done.6 = s32[2]{0:T(128)S(1)} copy-done((s32[2]{0:T(128)S(1)}, s32[2]{0:T(128)}, u32[]{:S(2)}) %copy-start.6) | copy-done | bytes 32
  6.9 0.0 copy-start.4
  6.9 2.5 %shard_map.82.own = bf16[16,1024]{1,0:T(8,128)(2,1)S(1)} custom-call(s32[2]{0:T(128)S(1)} %copy-done.6, f32[1,512]{1,0:T(1,128)S(1)} %copy-done.5, f32[8,20480]{1,0:T(8,128)S(1)} %copy-done.1, f32[1096,128]{1,0:T(8,128)S(1)} %copy-done.3, bf16[2,8,256,256]{3,2,1,0:T(8,128)(2,1)S(1)} %copy-done, bf16[640,512]{1,0:T(8,128)(2,1)S(1)} %copy-done.2), custom_call_target="tpu_custom_call" | custom-call | tf_op jit(solution)/shard_map/pallas_call | solution.py:342
  9.5 0.0 copy-done.4
  9.5 17.0 %shard_map.83 = bf16[64,32,128]{2,1,0:T(8,128)(2,1)S(1)} custom-call(s32[1,4,1]{2,1,0:T(4,128)S(1)} %copy.9.mask, bf16[16,1024]{1,0:T(8,128)(2,1)S(1)} %shard_map.82.own, bf16[1024,128]{1,0:T(8,128)(2,1)S(1)} %copy-done.4), custom_call_target="tpu_custom_call" | custom-call | tf_op jit(solution)/shard_map/pallas_call | solution.py:356
  26.4 0.8 %copy.12 = bf16[64,4,1,8,128]{4,3,2,1,0:T(8,128)(2,1)} copy(bf16[64,4,1,8,128]{4,3,2,1,0:T(8,128)(2,1)S(1)} %bitcast.3) | data formatting | bytes 1048576
Async XLA Ops:
  0.7 1.6 %copy-start = (bf16[2,8,256,256]{3,2,1,0:T(8,128)(2,1)S(1)}, bf16[2,8,256,256]{3,2,1,0:T(8,128)(2,1)}, u32[]{:S(2)}) copy-start(bf16[2,8,256,256]{3,2,1,0:T(8,128)(2,1)} %constant.12.clone.tables_hbm) | copy-start | bytes 6291460
  2.3 1.1 %copy-start.1 = (f32[8,20480]{1,0:T(8,128)S(1)}, f32[8,20480]{1,0:T(8,128)}, u32[]{:S(2)}) copy-start(f32[8,20480]{1,0:T(8,128)} %records_hbm.1) | copy-start | bytes 1966084
  3.4 1.1 %copy-start.2 = (bf16[640,512]{1,0:T(8,128)(2,1)S(1)}, bf16[640,512]{1,0:T(8,128)(2,1)}, u32[]{:S(2)}) copy-start(bf16[640,512]{1,0:T(8,128)(2,1)} %constant.13.clone.inside_hbm) | copy-start | bytes 1966084
  4.5 1.1 %copy-start.3 = (f32[1096,128]{1,0:T(8,128)S(1)}, f32[1096,128]{1,0:T(8,128)}, u32[]{:S(2)}) copy-start(f32[1096,128]{1,0:T(8,128)} %constant.11.clone.band_hbm) | copy-start | bytes 1683460
  5.6 0.7 %copy-start.5 = (f32[1,512]{1,0:T(1,128)S(1)}, f32[1,512]{1,0:T(1,128)}, u32[]{:S(2)}) copy-start(f32[1,512]{1,0:T(1,128)} %constant.10.clone.per_bin) | copy-start | bytes 6148
  6.2 0.7 %copy-start.6 = (s32[2]{0:T(128)S(1)}, s32[2]{0:T(128)}, u32[]{:S(2)}) copy-start(s32[2]{0:T(128)} %starts.1) | copy-start | bytes 28
  6.9 2.6 %copy-start.4 = (bf16[1024,128]{1,0:T(8,128)(2,1)S(1)}, bf16[1024,128]{1,0:T(8,128)(2,1)}, u32[]{:S(2)}) copy-start(bf16[1024,128]{1,0:T(8,128)(2,1)} %constant.14.clone.lags_hbm) | copy-start | bytes 786436

commit v2 on v1

--- a/solution.py
+++ b/solution.py
@@ -185,13 +185,14 @@
 
 
 def spectra_kernel(
-    starts, per_bin, records_hbm, band_hbm, tables_hbm, inside_hbm, out,
-    records, band, tables, inside, load_sem,
+    starts, records_hbm, band_hbm, tables_hbm, inside_hbm, per_bin_hbm, out,
+    records, band, tables, inside, per_bin, load_sem,
 ):
     loads = [
         pltpu.make_async_copy(a, b, load_sem.at[i])
         for i, (a, b) in enumerate(
-            [(records_hbm, records), (band_hbm, band), (tables_hbm, tables), (inside_hbm, inside)]
+            [(records_hbm, records), (band_hbm, band), (tables_hbm, tables), (inside_hbm, inside),
+             (per_bin_hbm, per_bin)]
         )
     ]
     for load in loads:
@@ -201,14 +202,18 @@
         loads[0].wait()
         loads[1].wait()
 
+    def last_wait():
+        loads[3].wait()
+        loads[4].wait()
+
     out[...] = whiten(
-        starts, records, band, tables, inside, per_bin, [first_wait, loads[2].wait, loads[3].wait]
+        starts, records, band, tables, inside, per_bin, [first_wait, loads[2].wait, last_wait]
     )
 
 
 def pair_kernel(
     n_src, n_rcv, mask, own, lags_hbm, out,
-    lags, src_buf, rcv_buf, src_f32, rcv_f32, cross, threshold,
+    lags, src_buf, rcv_buf, src_f32, rcv_buf2, cross_even, cross_odd, threshold,
     load_sem, src_send, src_recv, rcv_send, rcv_recv,
 ):
     me_s, me_r = lax.axis_index("src"), lax.axis_index("rcv")
@@ -248,7 +253,12 @@
         )
 
     def send_rcv(k, _):
-        rcv_copy(me_r, flip(me_r, k, rcv_bits)).start()
+        peer = flip(me_r, k, rcv_bits)
+
+        @pl.when(peer < me_r)
+        def _():
+            rcv_copy(me_r, peer).start()
+
         return 0
 
     def send_src(k, _):
@@ -261,75 +271,95 @@
     block_rows = n_src * CH
     for b in range(n_rcv):
         ids = lax.broadcasted_iota(jnp.int32, (CH, LAGS), 0) + b * block_rows + me_s * CH
-        threshold[CH * b : CH * (b + 1), :] = jnp.where(mask[0, b, 0] > 0, ids, -1)
+        threshold[CH * b : CH * (b + 1), :] = jnp.where(mask[0, b] > 0, ids, -1)
+
+    def clear_rcv(k, _):
+        rcv_buf[k] = jnp.zeros(rcv_buf.shape[1:], rcv_buf.dtype)
+        return 0
 
     def land_rcv(k, _):
-        peer = flip(me_r, k, rcv_bits)
-
-        @pl.when(k > 0)
-        def _():
-            rcv_copy(peer, peer).wait_recv()
-
-        held = rcv_buf[peer].astype(jnp.float32)
+        rcv_copy(k, k).wait_recv()
+        return 0
+
+    lax.fori_loop(0, me_r, clear_rcv, 0)
+    lax.fori_loop(me_r + 1, n_rcv, land_rcv, 0)
+    for b in range(0, n_rcv, 2):
         for w in range(WINDOWS):
-            rcv_f32[w, pl.ds(pl.multiple_of(peer * CH, CH), CH), :] = held[w * CH : (w + 1) * CH]
-        return 0
-
-    lax.fori_loop(0, n_rcv, land_rcv, 0)
+            at = slice(w * CH, (w + 1) * CH)
+            pair = [rcv_buf[b + i].astype(jnp.float32)[at] for i in range(2)]
+            rcv_buf2[w, b * CH : (b + 2) * CH, :] = jnp.concatenate(pair, axis=0).astype(jnp.bfloat16)
     load.wait()
 
     rows = n_rcv * CH
     part = min(rows, 32)
 
-    def per_source(k, _):
+    def products(k, cross):
         peer = flip(me_s, k, src_bits)
-
-        @pl.when(k > 0)
-        def _():
-            src_copy(peer, peer).wait_recv()
-
         src_f32[...] = src_buf[peer].astype(jnp.float32)
         for at in range(0, rows, part):
             for q in range(FB // LANES):
                 lo, hi = q * LANES, FB + q * LANES
                 held = [
-                    (rcv_f32[w, at : at + part, lo : lo + LANES], rcv_f32[w, at : at + part, hi : hi + LANES])
+                    (rcv_buf2[w, at : at + part, lo : lo + LANES], rcv_buf2[w, at : at + part, hi : hi + LANES])
                     for w in range(WINDOWS)
                 ]
                 for c in range(CH):
                     re = im = None
                     for w in range(WINDOWS):
                         row = w * CH + c
-                        s_re = src_f32[row : row + 1, lo : lo + LANES]
-                        s_im = src_f32[row : row + 1, hi : hi + LANES]
+                        s_re, s_im = [
+                            jnp.broadcast_to(src_f32[row : row + 1, x : x + LANES], (part, LANES)).astype(jnp.bfloat16)
+                            for x in (lo, hi)
+                        ]
                         r_re, r_im = held[w]
                         one = s_re * r_re + s_im * r_im
                         two = s_im * r_re - s_re * r_im
                         re = one if re is None else re + one
                         im = two if im is None else im + two
                     to = c * rows + at
-                    cross[to : to + part, lo : lo + LANES] = re.astype(jnp.bfloat16)
-                    cross[to : to + part, hi : hi + LANES] = im.astype(jnp.bfloat16)
-        lagged = dot(cross[...], lags[...])
+                    cross[to : to + part, lo : lo + LANES] = re
+                    cross[to : to + part, hi : hi + LANES] = im
+
+    def lagged(k, cross):
+        peer = flip(me_s, k, src_bits)
+        values = dot(cross[...], lags[...])
         first_id = me_r * block_rows + peer * CH
         for c in range(CH):
             keep = threshold[...] > first_id + c
-            value = jnp.where(keep, lagged[c * rows : (c + 1) * rows], 0.0)
+            value = jnp.where(keep, values[c * rows : (c + 1) * rows], 0.0)
             out[peer * CH + c] = value.astype(jnp.bfloat16)
-        return 0
-
-    lax.fori_loop(0, n_src, per_source, 0)
+
+    def arrive(k):
+        peer = flip(me_s, k, src_bits)
+        src_copy(peer, peer).wait_recv()
+
+    products(0, cross_even)
+
+    def two_sources(t, _):
+        arrive(2 * t + 1)
+        products(2 * t + 1, cross_odd)
+        lagged(2 * t, cross_even)
+        arrive(2 * t + 2)
+        products(2 * t + 2, cross_even)
+        lagged(2 * t + 1, cross_odd)
+        return 0
+
+    lax.fori_loop(0, n_src // 2 - 1, two_sources, 0)
+    arrive(n_src - 1)
+    products(n_src - 1, cross_odd)
+    lagged(n_src - 2, cross_even)
+    lagged(n_src - 1, cross_odd)
 
     def sent_src(k, _):
         src_copy(me_s, flip(me_s, k, src_bits)).wait_send()
         return 0
 
     def sent_rcv(k, _):
-        rcv_copy(me_r, flip(me_r, k, rcv_bits)).wait_send()
+        rcv_copy(me_r, k).wait_send()
         return 0
 
     lax.fori_loop(1, n_src, sent_src, 0)
-    lax.fori_loop(1, n_rcv, sent_rcv, 0)
+    lax.fori_loop(0, me_r, sent_rcv, 0)
 
 
 def on_device(n_src, n_rcv, records, starts, block_mask):
@@ -342,17 +372,18 @@
     own = pl.pallas_call(
         spectra_kernel,
         out_shape=jax.ShapeDtypeStruct(held, jnp.bfloat16),
-        in_specs=[smem, vmem] + [anywhere] * 4,
+        in_specs=[smem] + [anywhere] * 5,
         out_specs=vmem,
         scratch_shapes=[
             pltpu.VMEM(records.shape, jnp.float32),
             pltpu.VMEM(band.shape, jnp.float32),
             pltpu.VMEM(tables.shape, jnp.bfloat16),
             pltpu.VMEM(inside.shape, jnp.bfloat16),
-            pltpu.SemaphoreType.DMA((4,)),
+            pltpu.VMEM(per_bin.shape, jnp.float32),
+            pltpu.SemaphoreType.DMA((5,)),
         ],
-        compiler_params=pltpu.CompilerParams(vmem_limit_bytes=32 * 1024 * 1024),
-    )(starts, per_bin, records, band, tables, inside)
+        compiler_params=pltpu.CompilerParams(vmem_limit_bytes=60 * 1024 * 1024),
+    )(starts, records, band, tables, inside, per_bin)
     result = pl.pallas_call(
         functools.partial(pair_kernel, n_src, n_rcv),
         out_shape=jax.ShapeDtypeStruct((n_src * CH, rows, LAGS), jnp.bfloat16),
@@ -363,7 +394,8 @@
             pltpu.VMEM((n_src,) + held, jnp.bfloat16),
             pltpu.VMEM((n_rcv,) + held, jnp.bfloat16),
             pltpu.VMEM(held, jnp.float32),
-            pltpu.VMEM((WINDOWS, rows, 2 * FB), jnp.float32),
+            pltpu.VMEM((WINDOWS, rows, 2 * FB), jnp.bfloat16),
+            pltpu.VMEM((CH * rows, 2 * FB), jnp.bfloat16),
             pltpu.VMEM((CH * rows, 2 * FB), jnp.bfloat16),
             pltpu.VMEM((rows, LAGS), jnp.int32),
             pltpu.SemaphoreType.DMA,
@@ -373,9 +405,9 @@
             pltpu.SemaphoreType.DMA((n_rcv,)),
         ],
         compiler_params=pltpu.CompilerParams(
-            collective_id=0, has_side_effects=True, vmem_limit_bytes=32 * 1024 * 1024
+            collective_id=0, has_side_effects=True, vmem_limit_bytes=60 * 1024 * 1024
         ),
-    )(block_mask, own, lags)
+    )(block_mask.reshape(1, n_rcv), own, lags)
     return result.reshape(n_src * CH, n_rcv, 1, CH, LAGS)
 
 

time: 27.5 us -> 22.8 us (0.83)
  local copies, waits for them, and re-layouts: 7.69 us -> 1.87 us
  Pallas kernels: 19.5 us -> 20.7 us
    unnamed x16 -> x1, local copies, waits for them, and re-layouts: 7.69 us -> 1.87 us
    pallas_call x1, Pallas kernels: 2.54 us -> 4.01 us  [on_device(): pl.pallas_call(spectra_kernel, out_shape=jax.ShapeDtypeStruct(held, jnp.b...]
    pallas_call x1, Pallas kernels: 17 us -> 16.6 us  [on_device(): pl.pallas_call(functools.partial(pair_kernel, n_src, n_rcv), out_shape=ja...]
where the time goes in v2:
time: 22.8 us; the launch traced here: 22.5 us
  Pallas kernels  20.7 us (91%)
  local copies, waits for them, and re-layouts  1.87 us (8%)
    pallas_call x1, Pallas kernels, on_device(): pl.pallas_call(functools.partial(pair_kernel, n_src, n_rcv), out_shape=ja...  16.6 us
    pallas_call x1, Pallas kernels, on_device(): pl.pallas_call(spectra_kernel, out_shape=jax.ShapeDtypeStruct(held, jnp.b...  4.01 us
    unnamed x1, local copies, waits for them, and re-layouts  1.87 us

profile of v2, /device:TPU:0, one launch (start us, length us, event | category | flops | bytes accessed | tf_op | source)
XLA Modules:
  0.0 22.5 jit_solution(7189250178292943415)
XLA Ops:
  0.0 4.0 %shard_map.82.own = bf16[16,1024]{1,0:T(8,128)(2,1)} custom-call(s32[2]{0:T(128)} %starts.1, f32[8,20480]{1,0:T(8,128)} %records_hbm.1, f32[1096,128]{1,0:T(8,128)} %constant.10.clone.band_hbm, bf16[2,8,256,256]{3,2,1,0:T(8,128)(2,1)} %constant.11.clone.tables_hbm, bf16[640,512]{1,0:T(8,128)(2,1)} %constant.12.clone.inside_hbm, ...), custom_call_target="tpu_custom_call" | custom-call | tf_op jit(solution)/shard_map/pallas_call | solution.py:372
  4.0 16.6 %shard_map.83 = bf16[64,32,128]{2,1,0:T(8,128)(2,1)} custom-call(s32[1,4]{1,0:T(1,128)} %bitcast.5, bf16[16,1024]{1,0:T(8,128)(2,1)} %shard_map.82.own, bf16[1024,128]{1,0:T(8,128)(2,1)} %constant.14.clone.lags_hbm), custom_call_target="tpu_custom_call" | custom-call | tf_op jit(solution)/shard_map/pallas_call | solution.py:387
  20.7 1.9 %copy.11 = bf16[64,4,1,8,128]{4,3,2,1,0:T(8,128)(2,1)} copy(bf16[64,4,1,8,128]{4,3,2,1,0:T(8,128)(2,1)} %bitcast.4) | data formatting | bytes 1048576

commit v3 on v2

--- a/solution.py
+++ b/solution.py
@@ -20,6 +20,7 @@
 LANES = 128
 WINDOWS = 2
 CH = 8
+PAIR = 2 * CH
 
 CHUNKS = NT // LANES
 STRIDE = DEC * LANES
@@ -213,7 +214,7 @@
 
 def pair_kernel(
     n_src, n_rcv, mask, own, lags_hbm, out,
-    lags, src_buf, rcv_buf, src_f32, rcv_buf2, cross_even, cross_odd, threshold,
+    lags, src_buf, rcv_buf, src_f32, held_rcv, cross_even, cross_odd, threshold,
     load_sem, src_send, src_recv, rcv_send, rcv_recv,
 ):
     me_s, me_r = lax.axis_index("src"), lax.axis_index("rcv")
@@ -273,42 +274,55 @@
         ids = lax.broadcasted_iota(jnp.int32, (CH, LAGS), 0) + b * block_rows + me_s * CH
         threshold[CH * b : CH * (b + 1), :] = jnp.where(mask[0, b] > 0, ids, -1)
 
-    def clear_rcv(k, _):
-        rcv_buf[k] = jnp.zeros(rcv_buf.shape[1:], rcv_buf.dtype)
-        return 0
-
-    def land_rcv(k, _):
-        rcv_copy(k, k).wait_recv()
-        return 0
-
-    lax.fori_loop(0, me_r, clear_rcv, 0)
-    lax.fori_loop(me_r + 1, n_rcv, land_rcv, 0)
-    for b in range(0, n_rcv, 2):
+    load.wait()
+    units = n_src // 2
+    own_pair = me_r // 2
+
+    def clear(p, _):
+        for i in range(n_src * CH):
+            out[i, pl.ds(pl.multiple_of(p * PAIR, PAIR), PAIR), :] = jnp.zeros((PAIR, LAGS), out.dtype)
+        return 0
+
+    lax.fori_loop(0, own_pair, clear, 0)
+
+    def one_pair(p, _):
+        at = pl.ds(pl.multiple_of(p * PAIR, PAIR), PAIR)
+        for i in range(2):
+            block = 2 * p + i
+
+            @pl.when(block > me_r)
+            def _():
+                rcv_copy(block, block).wait_recv()
+
+            @pl.when(block < me_r)
+            def _():
+                rcv_buf[block] = jnp.zeros(rcv_buf.shape[1:], rcv_buf.dtype)
+
+        both = [rcv_buf[2 * p + i].astype(jnp.float32) for i in range(2)]
         for w in range(WINDOWS):
-            at = slice(w * CH, (w + 1) * CH)
-            pair = [rcv_buf[b + i].astype(jnp.float32)[at] for i in range(2)]
-            rcv_buf2[w, b * CH : (b + 2) * CH, :] = jnp.concatenate(pair, axis=0).astype(jnp.bfloat16)
-    load.wait()
-
-    rows = n_rcv * CH
-    part = min(rows, 32)
-
-    def products(k, cross):
-        peer = flip(me_s, k, src_bits)
-        src_f32[...] = src_buf[peer].astype(jnp.float32)
-        for at in range(0, rows, part):
+            rows = slice(w * CH, (w + 1) * CH)
+            held_rcv[w] = jnp.concatenate([x[rows] for x in both], axis=0).astype(jnp.bfloat16)
+
+        def arrive(u, first):
+            for i in range(first, 2):
+
+                @pl.when(p == own_pair)
+                def _():
+                    peer = flip(me_s, 2 * u + i, src_bits)
+                    src_copy(peer, peer).wait_recv()
+
+        def products(u, cross):
+            for i in range(2):
+                src_f32[i] = src_buf[flip(me_s, 2 * u + i, src_bits)].astype(jnp.float32)
             for q in range(FB // LANES):
-                lo, hi = q * LANES, FB + q * LANES
-                held = [
-                    (rcv_buf2[w, at : at + part, lo : lo + LANES], rcv_buf2[w, at : at + part, hi : hi + LANES])
-                    for w in range(WINDOWS)
-                ]
-                for c in range(CH):
+                lo, hi = slice(q * LANES, (q + 1) * LANES), slice(FB + q * LANES, FB + (q + 1) * LANES)
+                held = [(held_rcv[w, :, lo], held_rcv[w, :, hi]) for w in range(WINDOWS)]
+                for c in range(2 * CH):
                     re = im = None
                     for w in range(WINDOWS):
-                        row = w * CH + c
+                        row = slice(w * CH + c % CH, w * CH + c % CH + 1)
                         s_re, s_im = [
-                            jnp.broadcast_to(src_f32[row : row + 1, x : x + LANES], (part, LANES)).astype(jnp.bfloat16)
+                            jnp.broadcast_to(src_f32[c // CH, row, x], (PAIR, LANES)).astype(jnp.bfloat16)
                             for x in (lo, hi)
                         ]
                         r_re, r_im = held[w]
@@ -316,39 +330,38 @@
                         two = s_im * r_re - s_re * r_im
                         re = one if re is None else re + one
                         im = two if im is None else im + two
-                    to = c * rows + at
-                    cross[to : to + part, lo : lo + LANES] = re
-                    cross[to : to + part, hi : hi + LANES] = im
-
-    def lagged(k, cross):
-        peer = flip(me_s, k, src_bits)
-        values = dot(cross[...], lags[...])
-        first_id = me_r * block_rows + peer * CH
-        for c in range(CH):
-            keep = threshold[...] > first_id + c
-            value = jnp.where(keep, values[c * rows : (c + 1) * rows], 0.0)
-            out[peer * CH + c] = value.astype(jnp.bfloat16)
-
-    def arrive(k):
-        peer = flip(me_s, k, src_bits)
-        src_copy(peer, peer).wait_recv()
-
-    products(0, cross_even)
-
-    def two_sources(t, _):
-        arrive(2 * t + 1)
-        products(2 * t + 1, cross_odd)
-        lagged(2 * t, cross_even)
-        arrive(2 * t + 2)
-        products(2 * t + 2, cross_even)
-        lagged(2 * t + 1, cross_odd)
-        return 0
-
-    lax.fori_loop(0, n_src // 2 - 1, two_sources, 0)
-    arrive(n_src - 1)
-    products(n_src - 1, cross_odd)
-    lagged(n_src - 2, cross_even)
-    lagged(n_src - 1, cross_odd)
+                    cross[c * PAIR : (c + 1) * PAIR, lo] = re
+                    cross[c * PAIR : (c + 1) * PAIR, hi] = im
+
+        def lagged(u, cross):
+            values = dot(cross[...], lags[...])
+            limit = threshold[at, :]
+            for c in range(2 * CH):
+                row = flip(me_s, 2 * u + c // CH, src_bits) * CH + c % CH
+                keep = limit > me_r * block_rows + row
+                value = jnp.where(keep, values[c * PAIR : (c + 1) * PAIR], 0.0)
+                out[row, at, :] = value.astype(jnp.bfloat16)
+
+        arrive(0, 1)
+        products(0, cross_even)
+
+        def two_units(t, _):
+            arrive(2 * t + 1, 0)
+            products(2 * t + 1, cross_odd)
+            lagged(2 * t, cross_even)
+            arrive(2 * t + 2, 0)
+            products(2 * t + 2, cross_even)
+            lagged(2 * t + 1, cross_odd)
+            return 0
+
+        lax.fori_loop(0, units // 2 - 1, two_units, 0)
+        arrive(units - 1, 0)
+        products(units - 1, cross_odd)
+        lagged(units - 2, cross_even)
+        lagged(units - 1, cross_odd)
+        return 0
+
+    lax.fori_loop(own_pair, n_rcv // 2, one_pair, 0)
 
     def sent_src(k, _):
         src_copy(me_s, flip(me_s, k, src_bits)).wait_send()
@@ -393,10 +406,10 @@
             pltpu.VMEM(lags.shape, jnp.bfloat16),
             pltpu.VMEM((n_src,) + held, jnp.bfloat16),
             pltpu.VMEM((n_rcv,) + held, jnp.bfloat16),
-            pltpu.VMEM(held, jnp.float32),
-            pltpu.VMEM((WINDOWS, rows, 2 * FB), jnp.bfloat16),
-            pltpu.VMEM((CH * rows, 2 * FB), jnp.bfloat16),
-            pltpu.VMEM((CH * rows, 2 * FB), jnp.bfloat16),
+            pltpu.VMEM((2,) + held, jnp.float32),
+            pltpu.VMEM((WINDOWS, PAIR, 2 * FB), jnp.bfloat16),
+            pltpu.VMEM((2 * CH * PAIR, 2 * FB), jnp.bfloat16),
+            pltpu.VMEM((2 * CH * PAIR, 2 * FB), jnp.bfloat16),
             pltpu.VMEM((rows, LAGS), jnp.int32),
             pltpu.SemaphoreType.DMA,
             pltpu.SemaphoreType.DMA((n_src,)),
@@ -405,7 +418,7 @@
             pltpu.SemaphoreType.DMA((n_rcv,)),
         ],
         compiler_params=pltpu.CompilerParams(
-            collective_id=0, has_side_effects=True, vmem_limit_bytes=60 * 1024 * 1024
+            collective_id=0, has_side_effects=True, vmem_limit_bytes=24 * 1024 * 1024
         ),
     )(block_mask.reshape(1, n_rcv), own, lags)
     return result.reshape(n_src * CH, n_rcv, 1, CH, LAGS)

time: 22.8 us -> 20.2 us (0.89)
  Pallas kernels: 20.7 us -> 18.4 us
  local copies, waits for them, and re-layouts: 1.87 us -> 1.56 us
    pallas_call x1, Pallas kernels: 16.6 us -> 14.2 us  [on_device(): pl.pallas_call(functools.partial(pair_kernel, n_src, n_rcv), out_shape=ja...]
    unnamed x1 -> x7, local copies, waits for them, and re-layouts: 1.87 us -> 1.56 us
where the time goes in v3:
time: 20.2 us; the launch traced here: 20 us
  Pallas kernels  18.4 us (91%)
  local copies, waits for them, and re-layouts  1.56 us (8%)
    pallas_call x1, Pallas kernels, on_device(): pl.pallas_call(functools.partial(pair_kernel, n_src, n_rcv), out_shape=ja...  14.2 us
    pallas_call x1, Pallas kernels, on_device(): pl.pallas_call(spectra_kernel, out_shape=jax.ShapeDtypeStruct(held, jnp.b...  4.15 us
    unnamed x7, local copies, waits for them, and re-layouts  1.56 us

profile of v3, /device:TPU:0, one launch (start us, length us, event | category | flops | bytes accessed | tf_op | source)
XLA Modules:
  0.0 20.0 jit_solution(18049309821321065481)
XLA Ops:
  0.0 0.0 copy-start
  0.0 0.0 copy-start.2
  0.0 4.1 %shard_map.82.own = bf16[16,1024]{1,0:T(8,128)(2,1)} custom-call(s32[2]{0:T(128)} %starts.1, f32[8,20480]{1,0:T(8,128)} %records_hbm.1, f32[1096,128]{1,0:T(8,128)} %constant.10.clone.band_hbm, bf16[2,8,256,256]{3,2,1,0:T(8,128)(2,1)} %constant.11.clone.tables_hbm, bf16[640,512]{1,0:T(8,128)(2,1)} %constant.12.clone.inside_hbm, ...), custom_call_target="tpu_custom_call" | custom-call | tf_op jit(solution)/shard_map/pallas_call | solution.py:385
  4.2 0.0 copy-done
  4.2 0.0 copy-done.2
  4.2 0.0 copy-start.1
  4.2 0.7 %copy-done.1 = bf16[16,1024]{1,0:T(8,128)(2,1)S(1)} copy-done((bf16[16,1024]{1,0:T(8,128)(2,1)S(1)}, bf16[16,1024]{1,0:T(8,128)(2,1)}, u32[]{:S(2)}) %copy-start.1) | copy-done | bytes 32792
  4.9 14.2 %shard_map.83 = bf16[64,32,128]{2,1,0:T(8,128)(2,1)S(1)} custom-call(s32[1,4]{1,0:T(1,128)S(1)} %bitcast.5, bf16[16,1024]{1,0:T(8,128)(2,1)S(1)} %copy-done.1, bf16[1024,128]{1,0:T(8,128)(2,1)S(1)} %copy-done), custom_call_target="tpu_custom_call" | custom-call | tf_op jit(solution)/shard_map/pallas_call | solution.py:400
  19.2 0.8 %copy.11 = bf16[64,4,1,8,128]{4,3,2,1,0:T(8,128)(2,1)} copy(bf16[64,4,1,8,128]{4,3,2,1,0:T(8,128)(2,1)S(1)} %bitcast.4) | data formatting | bytes 1048576
Async XLA Ops:
  0.0 4.2 %copy-start = (bf16[1024,128]{1,0:T(8,128)(2,1)S(1)}, bf16[1024,128]{1,0:T(8,128)(2,1)}, u32[]{:S(2)}) copy-start(bf16[1024,128]{1,0:T(8,128)(2,1)} %constant.14.clone.lags_hbm) | copy-start | bytes 786436
  0.0 4.2 %copy-start.2 = (s32[1,4,1]{1,2,0:T(1,128)S(1)}, s32[1,4,1]{1,2,0:T(1,128)}, u32[]{:S(2)}) copy-start(s32[1,4,1]{1,2,0:T(1,128)} %param.10) | copy-start | bytes 52
  4.2 0.8 %copy-start.1 = (bf16[16,1024]{1,0:T(8,128)(2,1)S(1)}, bf16[16,1024]{1,0:T(8,128)(2,1)}, u32[]{:S(2)}) copy-start(bf16[16,1024]{1,0:T(8,128)(2,1)} %shard_map.82.own) | copy-start | bytes 98308

commit v4 on v3

--- a/solution.py
+++ b/solution.py
@@ -214,7 +214,7 @@
 
 def pair_kernel(
     n_src, n_rcv, mask, own, lags_hbm, out,
-    lags, src_buf, rcv_buf, src_f32, held_rcv, cross_even, cross_odd, threshold,
+    lags, src_buf, rcv_buf, held_rcv, cross_even, cross_odd, lag_even, lag_odd, threshold,
     load_sem, src_send, src_recv, rcv_send, rcv_recv,
 ):
     me_s, me_r = lax.axis_index("src"), lax.axis_index("rcv")
@@ -298,10 +298,12 @@
             def _():
                 rcv_buf[block] = jnp.zeros(rcv_buf.shape[1:], rcv_buf.dtype)
 
-        both = [rcv_buf[2 * p + i].astype(jnp.float32) for i in range(2)]
-        for w in range(WINDOWS):
-            rows = slice(w * CH, (w + 1) * CH)
-            held_rcv[w] = jnp.concatenate([x[rows] for x in both], axis=0).astype(jnp.bfloat16)
+        for i in range(2):
+            both = rcv_buf[2 * p + i].astype(jnp.float32)
+            for j in range(CH):
+                for w in range(WINDOWS):
+                    spread = jnp.broadcast_to(both[w * CH + j : w * CH + j + 1], (PAIR, 2 * FB))
+                    held_rcv[i * CH + j, w] = spread.astype(jnp.bfloat16)
 
         def arrive(u, first):
             for i in range(first, 2):
@@ -312,34 +314,32 @@
                     src_copy(peer, peer).wait_recv()
 
         def products(u, cross):
-            for i in range(2):
-                src_f32[i] = src_buf[flip(me_s, 2 * u + i, src_bits)].astype(jnp.float32)
+            both = [src_buf[flip(me_s, 2 * u + i, src_bits)].astype(jnp.float32) for i in range(2)]
+            held = [
+                jnp.concatenate([x[w * CH : (w + 1) * CH] for x in both], axis=0).astype(jnp.bfloat16)
+                for w in range(WINDOWS)
+            ]
             for q in range(FB // LANES):
                 lo, hi = slice(q * LANES, (q + 1) * LANES), slice(FB + q * LANES, FB + (q + 1) * LANES)
-                held = [(held_rcv[w, :, lo], held_rcv[w, :, hi]) for w in range(WINDOWS)]
-                for c in range(2 * CH):
+                for j in range(PAIR):
                     re = im = None
                     for w in range(WINDOWS):
-                        row = slice(w * CH + c % CH, w * CH + c % CH + 1)
-                        s_re, s_im = [
-                            jnp.broadcast_to(src_f32[c // CH, row, x], (PAIR, LANES)).astype(jnp.bfloat16)
-                            for x in (lo, hi)
-                        ]
-                        r_re, r_im = held[w]
+                        s_re, s_im = held[w][:, lo], held[w][:, hi]
+                        r_re, r_im = held_rcv[j, w, :, lo], held_rcv[j, w, :, hi]
                         one = s_re * r_re + s_im * r_im
                         two = s_im * r_re - s_re * r_im
                         re = one if re is None else re + one
                         im = two if im is None else im + two
-                    cross[c * PAIR : (c + 1) * PAIR, lo] = re
-                    cross[c * PAIR : (c + 1) * PAIR, hi] = im
-
-        def lagged(u, cross):
-            values = dot(cross[...], lags[...])
+                    cross[j * PAIR : (j + 1) * PAIR, lo] = re
+                    cross[j * PAIR : (j + 1) * PAIR, hi] = im
+
+        def lagged(u, cross, values):
+            values[...] = dot(cross[...], lags[...])
             limit = threshold[at, :]
             for c in range(2 * CH):
                 row = flip(me_s, 2 * u + c // CH, src_bits) * CH + c % CH
                 keep = limit > me_r * block_rows + row
-                value = jnp.where(keep, values[c * PAIR : (c + 1) * PAIR], 0.0)
+                value = jnp.where(keep, values[pl.ds(c, PAIR, stride=PAIR), :], 0.0)
                 out[row, at, :] = value.astype(jnp.bfloat16)
 
         arrive(0, 1)
@@ -348,17 +348,17 @@
         def two_units(t, _):
             arrive(2 * t + 1, 0)
             products(2 * t + 1, cross_odd)
-            lagged(2 * t, cross_even)
+            lagged(2 * t, cross_even, lag_even)
             arrive(2 * t + 2, 0)
             products(2 * t + 2, cross_even)
-            lagged(2 * t + 1, cross_odd)
+            lagged(2 * t + 1, cross_odd, lag_odd)
             return 0
 
         lax.fori_loop(0, units // 2 - 1, two_units, 0)
         arrive(units - 1, 0)
         products(units - 1, cross_odd)
-        lagged(units - 2, cross_even)
-        lagged(units - 1, cross_odd)
+        lagged(units - 2, cross_even, lag_even)
+        lagged(units - 1, cross_odd, lag_odd)
         return 0
 
     lax.fori_loop(own_pair, n_rcv // 2, one_pair, 0)
@@ -406,10 +406,11 @@
             pltpu.VMEM(lags.shape, jnp.bfloat16),
             pltpu.VMEM((n_src,) + held, jnp.bfloat16),
             pltpu.VMEM((n_rcv,) + held, jnp.bfloat16),
-            pltpu.VMEM((2,) + held, jnp.float32),
-            pltpu.VMEM((WINDOWS, PAIR, 2 * FB), jnp.bfloat16),
-            pltpu.VMEM((2 * CH * PAIR, 2 * FB), jnp.bfloat16),
-            pltpu.VMEM((2 * CH * PAIR, 2 * FB), jnp.bfloat16),
+            pltpu.VMEM((PAIR, WINDOWS, PAIR, 2 * FB), jnp.bfloat16),
+            pltpu.VMEM((PAIR * PAIR, 2 * FB), jnp.bfloat16),
+            pltpu.VMEM((PAIR * PAIR, 2 * FB), jnp.bfloat16),
+            pltpu.VMEM((PAIR * PAIR, LAGS), jnp.float32),
+            pltpu.VMEM((PAIR * PAIR, LAGS), jnp.float32),
             pltpu.VMEM((rows, LAGS), jnp.int32),
             pltpu.SemaphoreType.DMA,
             pltpu.SemaphoreType.DMA((n_src,)),

time: 20.2 us -> 20.5 us (1.015)
  Pallas kernels: 18.4 us -> 18.7 us
    pallas_call x1, Pallas kernels: 14.2 us -> 14.5 us  [on_device(): pl.pallas_call(functools.partial(pair_kernel, n_src, n_rcv), out_shape=ja...]
where the time goes in v4:
time: 20.5 us; the launch traced here: 20.3 us
  Pallas kernels  18.7 us (91%)
  local copies, waits for them, and re-layouts  1.56 us (8%)
    pallas_call x1, Pallas kernels, on_device(): pl.pallas_call(functools.partial(pair_kernel, n_src, n_rcv), out_shape=ja...  14.5 us
    pallas_call x1, Pallas kernels, on_device(): pl.pallas_call(spectra_kernel, out_shape=jax.ShapeDtypeStruct(held, jnp.b...  4.15 us
    unnamed x7, local copies, waits for them, and re-layouts  1.56 us

profile of v4, /device:TPU:0, one launch (start us, length us, event | category | flops | bytes accessed | tf_op | source)
XLA Modules:
  0.0 20.3 jit_solution(8577747891365957648)
XLA Ops:
  0.0 0.0 copy-start
  0.0 0.0 copy-start.2
  0.0 4.1 %shard_map.82.own = bf16[16,1024]{1,0:T(8,128)(2,1)} custom-call(s32[2]{0:T(128)} %starts.1, f32[8,20480]{1,0:T(8,128)} %records_hbm.1, f32[1096,128]{1,0:T(8,128)} %constant.10.clone.band_hbm, bf16[2,8,256,256]{3,2,1,0:T(8,128)(2,1)} %constant.11.clone.tables_hbm, bf16[640,512]{1,0:T(8,128)(2,1)} %constant.12.clone.inside_hbm, ...), custom_call_target="tpu_custom_call" | custom-call | tf_op jit(solution)/shard_map/pallas_call | solution.py:385
  4.2 0.0 copy-done
  4.2 0.0 copy-done.2
  4.2 0.0 copy-start.1
  4.2 0.7 %copy-done.1 = bf16[16,1024]{1,0:T(8,128)(2,1)S(1)} copy-done((bf16[16,1024]{1,0:T(8,128)(2,1)S(1)}, bf16[16,1024]{1,0:T(8,128)(2,1)}, u32[]{:S(2)}) %copy-start.1) | copy-done | bytes 32792
  4.9 14.5 %shard_map.83 = bf16[64,32,128]{2,1,0:T(8,128)(2,1)S(1)} custom-call(s32[1,4]{1,0:T(1,128)S(1)} %bitcast.5, bf16[16,1024]{1,0:T(8,128)(2,1)S(1)} %copy-done.1, bf16[1024,128]{1,0:T(8,128)(2,1)S(1)} %copy-done), custom_call_target="tpu_custom_call" | custom-call | tf_op jit(solution)/shard_map/pallas_call | solution.py:400
  19.5 0.8 %copy.11 = bf16[64,4,1,8,128]{4,3,2,1,0:T(8,128)(2,1)} copy(bf16[64,4,1,8,128]{4,3,2,1,0:T(8,128)(2,1)S(1)} %bitcast.4) | data formatting | bytes 1048576
Async XLA Ops:
  0.0 4.2 %copy-start = (bf16[1024,128]{1,0:T(8,128)(2,1)S(1)}, bf16[1024,128]{1,0:T(8,128)(2,1)}, u32[]{:S(2)}) copy-start(bf16[1024,128]{1,0:T(8,128)(2,1)} %constant.14.clone.lags_hbm) | copy-start | bytes 786436
  0.0 4.2 %copy-start.2 = (s32[1,4,1]{1,2,0:T(1,128)S(1)}, s32[1,4,1]{1,2,0:T(1,128)}, u32[]{:S(2)}) copy-start(s32[1,4,1]{1,2,0:T(1,128)} %param.10) | copy-start | bytes 52
  4.2 0.8 %copy-start.1 = (bf16[16,1024]{1,0:T(8,128)(2,1)S(1)}, bf16[16,1024]{1,0:T(8,128)(2,1)}, u32[]{:S(2)}) copy-start(bf16[16,1024]{1,0:T(8,128)(2,1)} %shard_map.82.own) | copy-start | bytes 98308

commit v5 on v3

--- a/solution.py
+++ b/solution.py
@@ -198,7 +198,6 @@
     ]
     for load in loads:
         load.start()
-
     def first_wait():
         loads[0].wait()
         loads[1].wait()
@@ -215,31 +214,38 @@
 def pair_kernel(
     n_src, n_rcv, mask, own, lags_hbm, out,
     lags, src_buf, rcv_buf, src_f32, held_rcv, cross_even, cross_odd, threshold,
-    load_sem, src_send, src_recv, rcv_send, rcv_recv,
+    load_sem, own_sem, src_send, fwd_send, src_recv, rcv_send, rcv_recv,
 ):
     me_s, me_r = lax.axis_index("src"), lax.axis_index("rcv")
     src_bits, rcv_bits = n_src.bit_length() - 1, n_rcv.bit_length() - 1
     load = pltpu.make_async_copy(lags_hbm, lags, load_sem)
     load.start()
+    places = [
+        pltpu.make_async_copy(own, src_buf.at[me_s], own_sem.at[0]),
+        pltpu.make_async_copy(own, rcv_buf.at[me_r], own_sem.at[1]),
+    ]
+    for place in places:
+        place.start()
 
     barrier = pltpu.get_barrier_semaphore()
 
+    sibling = flip(me_s, 1, src_bits)
+
     def greet_src(k, _):
-        peer = flip(me_s, k, src_bits)
+        peer = flip(me_s, 2 * k, src_bits)
         pl.semaphore_signal(barrier, inc=1, device_id={"src": peer}, device_id_type=MESH)
         return 0
 
     def greet_rcv(k, _):
-        peer = flip(me_r, k, rcv_bits)
-        pl.semaphore_signal(barrier, inc=1, device_id={"rcv": peer}, device_id_type=MESH)
-        return 0
-
-    lax.fori_loop(1, n_src, greet_src, 0)
-    lax.fori_loop(1, n_rcv, greet_rcv, 0)
-
-    src_buf[me_s] = own[...]
-    rcv_buf[me_r] = own[...]
-    pl.semaphore_wait(barrier, n_src + n_rcv - 2)
+        pl.semaphore_signal(barrier, inc=1, device_id={"rcv": k}, device_id_type=MESH)
+        return 0
+
+    pl.semaphore_signal(barrier, inc=1, device_id={"src": sibling}, device_id_type=MESH)
+    lax.fori_loop(1, n_src // 2, greet_src, 0)
+    lax.fori_loop(me_r + 1, n_rcv, greet_rcv, 0)
+    pl.semaphore_wait(barrier, n_src // 2 + me_r)
+    for place in places:
+        place.wait()
 
     def src_copy(slot, peer):
         return pltpu.make_async_remote_copy(
@@ -247,6 +253,12 @@
             recv_sem=src_recv.at[slot], device_id={"src": peer}, device_id_type=MESH,
         )
 
+    def forward(slot):
+        return pltpu.make_async_remote_copy(
+            src_ref=src_buf.at[slot], dst_ref=src_buf.at[slot], send_sem=fwd_send.at[slot],
+            recv_sem=src_recv.at[slot], device_id={"src": sibling}, device_id_type=MESH,
+        )
+
     def rcv_copy(slot, peer):
         return pltpu.make_async_remote_copy(
             src_ref=rcv_buf.at[slot], dst_ref=rcv_buf.at[slot], send_sem=rcv_send.at[peer],
@@ -254,20 +266,16 @@
         )
 
     def send_rcv(k, _):
-        peer = flip(me_r, k, rcv_bits)
-
-        @pl.when(peer < me_r)
-        def _():
-            rcv_copy(me_r, peer).start()
-
+        rcv_copy(me_r, me_r - 1 - k).start()
         return 0
 
     def send_src(k, _):
-        src_copy(me_s, flip(me_s, k, src_bits)).start()
-        return 0
-
-    lax.fori_loop(1, n_rcv, send_rcv, 0)
-    lax.fori_loop(1, n_src, send_src, 0)
+        src_copy(me_s, flip(me_s, 2 * k, src_bits)).start()
+        return 0
+
+    lax.fori_loop(1, n_src // 2, send_src, 0)
+    lax.fori_loop(0, me_r, send_rcv, 0)
+    src_copy(me_s, sibling).start()
 
     block_rows = n_src * CH
     for b in range(n_rcv):
@@ -303,13 +311,26 @@
             rows = slice(w * CH, (w + 1) * CH)
             held_rcv[w] = jnp.concatenate([x[rows] for x in both], axis=0).astype(jnp.bfloat16)
 
-        def arrive(u, first):
-            for i in range(first, 2):
-
-                @pl.when(p == own_pair)
-                def _():
-                    peer = flip(me_s, 2 * u + i, src_bits)
-                    src_copy(peer, peer).wait_recv()
+        def land(k):
+            peer = flip(me_s, k, src_bits)
+            src_copy(peer, peer).wait_recv()
+            forward(peer).start()
+
+        def arrive(u):
+            first = p == own_pair
+
+            @pl.when(first & (u == 1))
+            def _():
+                land(2)
+
+            @pl.when(first & (u > 0) & (u < units - 1))
+            def _():
+                land(2 * u + 2)
+
+            @pl.when(first)
+            def _():
+                peer = flip(me_s, 2 * u + 1, src_bits)
+                src_copy(peer, peer).wait_recv()
 
         def products(u, cross):
             for i in range(2):
@@ -342,20 +363,20 @@
                 value = jnp.where(keep, values[c * PAIR : (c + 1) * PAIR], 0.0)
                 out[row, at, :] = value.astype(jnp.bfloat16)
 
-        arrive(0, 1)
+        arrive(0)
         products(0, cross_even)
 
         def two_units(t, _):
-            arrive(2 * t + 1, 0)
+            arrive(2 * t + 1)
             products(2 * t + 1, cross_odd)
             lagged(2 * t, cross_even)
-            arrive(2 * t + 2, 0)
+            arrive(2 * t + 2)
             products(2 * t + 2, cross_even)
             lagged(2 * t + 1, cross_odd)
             return 0
 
         lax.fori_loop(0, units // 2 - 1, two_units, 0)
-        arrive(units - 1, 0)
+        arrive(units - 1)
         products(units - 1, cross_odd)
         lagged(units - 2, cross_even)
         lagged(units - 1, cross_odd)
@@ -364,14 +385,17 @@
     lax.fori_loop(own_pair, n_rcv // 2, one_pair, 0)
 
     def sent_src(k, _):
-        src_copy(me_s, flip(me_s, k, src_bits)).wait_send()
+        peer = flip(me_s, 2 * k, src_bits)
+        src_copy(me_s, peer).wait_send()
+        forward(peer).wait_send()
         return 0
 
     def sent_rcv(k, _):
         rcv_copy(me_r, k).wait_send()
         return 0
 
-    lax.fori_loop(1, n_src, sent_src, 0)
+    src_copy(me_s, sibling).wait_send()
+    lax.fori_loop(1, n_src // 2, sent_src, 0)
     lax.fori_loop(0, me_r, sent_rcv, 0)
 
 
@@ -400,7 +424,7 @@
     result = pl.pallas_call(
         functools.partial(pair_kernel, n_src, n_rcv),
         out_shape=jax.ShapeDtypeStruct((n_src * CH, rows, LAGS), jnp.bfloat16),
-        in_specs=[smem, vmem, anywhere],
+        in_specs=[smem, anywhere, anywhere],
         out_specs=vmem,
         scratch_shapes=[
             pltpu.VMEM(lags.shape, jnp.bfloat16),
@@ -412,6 +436,8 @@
             pltpu.VMEM((2 * CH * PAIR, 2 * FB), jnp.bfloat16),
             pltpu.VMEM((rows, LAGS), jnp.int32),
             pltpu.SemaphoreType.DMA,
+            pltpu.SemaphoreType.DMA((2,)),
+            pltpu.SemaphoreType.DMA((n_src,)),
             pltpu.SemaphoreType.DMA((n_src,)),
             pltpu.SemaphoreType.DMA((n_src,)),
             pltpu.SemaphoreType.DMA((n_rcv,)),

time: 20.2 us -> 19.9 us (0.985)
  Pallas kernels: 18.4 us -> 18.1 us
    pallas_call x1, Pallas kernels: 14.2 us -> 14 us  [on_device(): pl.pallas_call(functools.partial(pair_kernel, n_src, n_rcv), out_shape=ja...]
where the time goes in v5:
time: 19.9 us; the launch traced here: 19.7 us
  Pallas kernels  18.1 us (91%)
  local copies, waits for them, and re-layouts  1.56 us (8%)
    pallas_call x1, Pallas kernels, on_device(): pl.pallas_call(functools.partial(pair_kernel, n_src, n_rcv), out_shape=ja...  14 us
    pallas_call x1, Pallas kernels, on_device(): pl.pallas_call(spectra_kernel, out_shape=jax.ShapeDtypeStruct(held, jnp.b...  4.15 us
    unnamed x7, local copies, waits for them, and re-layouts  1.56 us

profile of v5, /device:TPU:0, one launch (start us, length us, event | category | flops | bytes accessed | tf_op | source)
XLA Modules:
  0.0 19.7 jit_solution(10240110541282370123)
XLA Ops:
  0.0 0.0 copy-start
  0.0 0.0 copy-start.2
  0.0 4.1 %shard_map.82.own = bf16[16,1024]{1,0:T(8,128)(2,1)} custom-call(s32[2]{0:T(128)} %starts.1, f32[8,20480]{1,0:T(8,128)} %records_hbm.1, f32[1096,128]{1,0:T(8,128)} %constant.10.clone.band_hbm, bf16[2,8,256,256]{3,2,1,0:T(8,128)(2,1)} %constant.11.clone.tables_hbm, bf16[640,512]{1,0:T(8,128)(2,1)} %constant.12.clone.inside_hbm, ...), custom_call_target="tpu_custom_call" | custom-call | tf_op jit(solution)/shard_map/pallas_call | solution.py:409
  4.2 0.0 copy-done
  4.2 0.0 copy-done.2
  4.2 0.0 copy-start.1
  4.2 0.7 %copy-done.1 = bf16[16,1024]{1,0:T(8,128)(2,1)S(1)} copy-done((bf16[16,1024]{1,0:T(8,128)(2,1)S(1)}, bf16[16,1024]{1,0:T(8,128)(2,1)}, u32[]{:S(2)}) %copy-start.1) | copy-done | bytes 32792
  4.9 14.0 %shard_map.83 = bf16[64,32,128]{2,1,0:T(8,128)(2,1)S(1)} custom-call(s32[1,4]{1,0:T(1,128)S(1)} %bitcast.5, bf16[16,1024]{1,0:T(8,128)(2,1)S(1)} %copy-done.1, bf16[1024,128]{1,0:T(8,128)(2,1)S(1)} %copy-done), custom_call_target="tpu_custom_call" | custom-call | tf_op jit(solution)/shard_map/pallas_call | solution.py:424
  18.9 0.8 %copy.11 = bf16[64,4,1,8,128]{4,3,2,1,0:T(8,128)(2,1)} copy(bf16[64,4,1,8,128]{4,3,2,1,0:T(8,128)(2,1)S(1)} %bitcast.4) | data formatting | bytes 1048576
Async XLA Ops:
  0.0 4.2 %copy-start = (bf16[1024,128]{1,0:T(8,128)(2,1)S(1)}, bf16[1024,128]{1,0:T(8,128)(2,1)}, u32[]{:S(2)}) copy-start(bf16[1024,128]{1,0:T(8,128)(2,1)} %constant.14.clone.lags_hbm) | copy-start | bytes 786436
  0.0 4.2 %copy-start.2 = (s32[1,4,1]{1,2,0:T(1,128)S(1)}, s32[1,4,1]{1,2,0:T(1,128)}, u32[]{:S(2)}) copy-start(s32[1,4,1]{1,2,0:T(1,128)} %param.10) | copy-start | bytes 52
  4.2 0.8 %copy-start.1 = (bf16[16,1024]{1,0:T(8,128)(2,1)S(1)}, bf16[16,1024]{1,0:T(8,128)(2,1)}, u32[]{:S(2)}) copy-start(bf16[16,1024]{1,0:T(8,128)(2,1)} %shard_map.82.own) | copy-start | bytes 98308

commit v6 on v5

--- a/solution.py
+++ b/solution.py
@@ -408,7 +408,7 @@
     anywhere = pl.BlockSpec(memory_space=pl.ANY)
     own = pl.pallas_call(
         spectra_kernel,
-        out_shape=jax.ShapeDtypeStruct(held, jnp.bfloat16),
+        out_shape=pltpu.VMEM(held, jnp.bfloat16),
         in_specs=[smem] + [anywhere] * 5,
         out_specs=vmem,
         scratch_shapes=[

time: 19.9 us -> 18.5 us (0.930)
  local copies, waits for them, and re-layouts: 1.56 us -> 0.8 us
  Pallas kernels: 18.1 us -> 17.5 us
    unnamed x7 -> x5, local copies, waits for them, and re-layouts: 1.56 us -> 0.8 us
    pallas_call x1, Pallas kernels: 4.15 us -> 3.53 us  [on_device(): pl.pallas_call(spectra_kernel, out_shape=pltpu.VMEM(held, jnp.bfloat16),...]
where the time goes in v6:
time: 18.5 us; the launch traced here: 18.4 us
  Pallas kernels  17.5 us (95%)
  local copies, waits for them, and re-layouts  0.8 us (4%)
    pallas_call x1, Pallas kernels, on_device(): pl.pallas_call(functools.partial(pair_kernel, n_src, n_rcv), out_shape=ja...  14 us
    pallas_call x1, Pallas kernels, on_device(): pl.pallas_call(spectra_kernel, out_shape=pltpu.VMEM(held, jnp.bfloat16),...  3.53 us
    unnamed x5, local copies, waits for them, and re-layouts  0.8 us

profile of v6, /device:TPU:0, one launch (start us, length us, event | category | flops | bytes accessed | tf_op | source)
XLA Modules:
  0.0 18.4 jit_solution(852996158384982362)
XLA Ops:
  0.0 0.0 copy-start
  0.0 0.0 copy-start.1
  0.0 3.5 %shard_map.82.own = bf16[16,1024]{1,0:T(8,128)(2,1)S(1)} custom-call(s32[2]{0:T(128)} %starts.1, f32[8,20480]{1,0:T(8,128)} %records_hbm.1, f32[1096,128]{1,0:T(8,128)} %constant.10.clone.band_hbm, bf16[2,8,256,256]{3,2,1,0:T(8,128)(2,1)} %constant.11.clone.tables_hbm, bf16[640,512]{1,0:T(8,128)(2,1)} %constant.12.clone.inside_hbm, ...), custom_call_target="tpu_custom_call" | custom-call | tf_op jit(solution)/shard_map/pallas_call | solution.py:409
  3.5 0.0 copy-done
  3.6 0.0 copy-done.1
  3.6 14.0 %shard_map.83 = bf16[64,32,128]{2,1,0:T(8,128)(2,1)S(1)} custom-call(s32[1,4]{1,0:T(1,128)S(1)} %bitcast.5, bf16[16,1024]{1,0:T(8,128)(2,1)S(1)} %shard_map.82.own, bf16[1024,128]{1,0:T(8,128)(2,1)S(1)} %copy-done), custom_call_target="tpu_custom_call" | custom-call | tf_op jit(solution)/shard_map/pallas_call | solution.py:424
  17.6 0.8 %copy.11 = bf16[64,4,1,8,128]{4,3,2,1,0:T(8,128)(2,1)} copy(bf16[64,4,1,8,128]{4,3,2,1,0:T(8,128)(2,1)S(1)} %bitcast.4) | data formatting | bytes 1048576
Async XLA Ops:
  0.0 3.5 %copy-start = (bf16[1024,128]{1,0:T(8,128)(2,1)S(1)}, bf16[1024,128]{1,0:T(8,128)(2,1)}, u32[]{:S(2)}) copy-start(bf16[1024,128]{1,0:T(8,128)(2,1)} %constant.14.clone.lags_hbm) | copy-start | bytes 786436
  0.0 3.6 %copy-start.1 = (s32[1,4,1]{1,2,0:T(1,128)S(1)}, s32[1,4,1]{1,2,0:T(1,128)}, u32[]{:S(2)}) copy-start(s32[1,4,1]{1,2,0:T(1,128)} %param.10) | copy-start | bytes 52

commit v7 on v6

--- a/solution.py
+++ b/solution.py
@@ -266,15 +266,15 @@
         )
 
     def send_rcv(k, _):
-        rcv_copy(me_r, me_r - 1 - k).start()
+        rcv_copy(me_r, k).start()
         return 0
 
     def send_src(k, _):
         src_copy(me_s, flip(me_s, 2 * k, src_bits)).start()
         return 0
 
+    lax.fori_loop(0, me_r, send_rcv, 0)
     lax.fori_loop(1, n_src // 2, send_src, 0)
-    lax.fori_loop(0, me_r, send_rcv, 0)
     src_copy(me_s, sibling).start()
 
     block_rows = n_src * CH

time: 18.5 us -> 18.4 us (level)
  no operation moved by 1% of the time
where the time goes in v7:
time: 18.4 us; the launch traced here: 18.2 us
  Pallas kernels  17.4 us (95%)
  local copies, waits for them, and re-layouts  0.8 us (4%)
    pallas_call x1, Pallas kernels, on_device(): pl.pallas_call(functools.partial(pair_kernel, n_src, n_rcv), out_shape=ja...  13.9 us
    pallas_call x1, Pallas kernels, on_device(): pl.pallas_call(spectra_kernel, out_shape=pltpu.VMEM(held, jnp.bfloat16),...  3.53 us
    unnamed x5, local copies, waits for them, and re-layouts  0.8 us

profile of v7, /device:TPU:0, one launch (start us, length us, event | category | flops | bytes accessed | tf_op | source)
XLA Modules:
  0.0 18.2 jit_solution(7651778198047737132)
XLA Ops:
  0.0 0.0 copy-start
  0.0 0.0 copy-start.1
  0.0 3.5 %shard_map.82.own = bf16[16,1024]{1,0:T(8,128)(2,1)S(1)} custom-call(s32[2]{0:T(128)} %starts.1, f32[8,20480]{1,0:T(8,128)} %records_hbm.1, f32[1096,128]{1,0:T(8,128)} %constant.10.clone.band_hbm, bf16[2,8,256,256]{3,2,1,0:T(8,128)(2,1)} %constant.11.clone.tables_hbm, bf16[640,512]{1,0:T(8,128)(2,1)} %constant.12.clone.inside_hbm, ...), custom_call_target="tpu_custom_call" | custom-call | tf_op jit(solution)/shard_map/pallas_call | solution.py:409
  3.5 0.0 copy-done
  3.6 0.0 copy-done.1
  3.6 13.9 %shard_map.83 = bf16[64,32,128]{2,1,0:T(8,128)(2,1)S(1)} custom-call(s32[1,4]{1,0:T(1,128)S(1)} %bitcast.5, bf16[16,1024]{1,0:T(8,128)(2,1)S(1)} %shard_map.82.own, bf16[1024,128]{1,0:T(8,128)(2,1)S(1)} %copy-done), custom_call_target="tpu_custom_call" | custom-call | tf_op jit(solution)/shard_map/pallas_call | solution.py:424
  17.4 0.8 %copy.11 = bf16[64,4,1,8,128]{4,3,2,1,0:T(8,128)(2,1)} copy(bf16[64,4,1,8,128]{4,3,2,1,0:T(8,128)(2,1)S(1)} %bitcast.4) | data formatting | bytes 1048576
Async XLA Ops:
  0.0 3.5 %copy-start = (bf16[1024,128]{1,0:T(8,128)(2,1)S(1)}, bf16[1024,128]{1,0:T(8,128)(2,1)}, u32[]{:S(2)}) copy-start(bf16[1024,128]{1,0:T(8,128)(2,1)} %constant.14.clone.lags_hbm) | copy-start | bytes 786436
  0.0 3.6 %copy-start.1 = (s32[1,4,1]{1,2,0:T(1,128)S(1)}, s32[1,4,1]{1,2,0:T(1,128)}, u32[]{:S(2)}) copy-start(s32[1,4,1]{1,2,0:T(1,128)} %param.10) | copy-start | bytes 52
